TPU v7x, 128 devices: a whole 4x4x4 slice. The times are simulated.
128 devices in a mesh: depth: 4 (over z), tile: 32 (over y, x, core).
Axes of the slice: x: 4, y: 4, z: 4, core: 2. Of those that a mesh axis runs over, the one named last changes fastest.
Arguments:
- features: bfloat16 [1024, 32, 512], P(('depth', 'tile')), may hold values from -6 to 6
- cotangent: bfloat16 [1024, 32, 512], P(('depth', 'tile')), may hold values from -6 to 6
- first_weight: bfloat16 [27, 32, 32], replicated, may hold values from -0.21875 to 0.21875
- second_weight: bfloat16 [27, 32, 32], replicated, may hold values from -0.21875 to 0.21875
- neighbours: int32 [1024, 26], P(('depth', 'tile')), may hold values from -1 to 15
- send_depth: int32 [128, 2, 2], P(('depth', 'tile')), may hold values from 0 to 7
- send_tile: int32 [128, 2, 2], P(('depth', 'tile')), may hold values from 0 to 11
- worker_tile: int32 [1024, 1], P(('depth', 'tile')), may hold values from 0 to 31; in each aligned block of 8 rows (0 to 7, 8 to 15, ...) at most 2 rows name the same one
Outputs:
- moved_grad: bfloat16 [8192, 32, 512], P(('depth', 'tile'))
- grad_weights: float32 [2, 27, 32, 32], replicated
Inputs may be any that keep to these rules, and one draw needn't show every extreme that they name: `neighbours`: lookup entries, -1 where no active brick is at that offset. `send_depth`: brick slots of the sending device. `send_tile`: entries of the sending device's depth-section lookup. `worker_tile`: at most 2 bricks of one device name the same tile, and this is reached.
All inputs are finite; a program needn't handle non-finite values.
Results may differ from a plain program's by a relative error of at most 0.0032.
Values may be sent and summed in bfloat16 or wider, within the bound.
A program may use at most 256 MiB of HBM per device.

v0:
```python
import jax
import jax.numpy as jnp
from jax import lax
from jax.sharding import PartitionSpec as P

BS = 8


brick_block = 8


def extended(x, sides, width, wrap):
    for axis, dim in sides:
        size, length = (lax.axis_size(axis), x.shape[dim])
        up = [(i, (i + 1) % size) for i in range(size if wrap else size - 1)]
        down = [(j, i) for i, j in up]
        last = lax.slice_in_dim(x, length - width, length, axis=dim)
        initial = lax.slice_in_dim(x, 0, width, axis=dim)
        before = lax.ppermute(last, axis, up)
        after = lax.ppermute(initial, axis, down)
        x = jnp.concatenate([before, x, after], axis=dim)
    return x


def silu_grad(values):
    sigma = jax.nn.sigmoid(values)
    return sigma * (1.0 + values * (1.0 - sigma))


def lookup_rows(own_rows, send_depth, send_tile):
    outgoing = jnp.stack(
        [jnp.take(own_rows, send_depth[0, 0], axis=0), jnp.take(own_rows, send_depth[0, 1], axis=0)]
    )
    arrived = extended(outgoing, (("depth", 0),), 1, False)
    arrived = jnp.concatenate([arrived[0], arrived[3]], 0)
    section_one = jnp.concatenate([own_rows, arrived], 0)
    leaving = jnp.stack(
        [
            jnp.take(section_one, send_tile[0, 0], axis=0),
            jnp.take(section_one, send_tile[0, 1], axis=0),
        ]
    )
    reached = extended(leaving, (("tile", 0),), 1, True)
    reached = jnp.concatenate([reached[0], reached[3]], 0)
    zero_brick = jnp.zeros_like(own_rows[:1])
    return jnp.concatenate([section_one, reached, zero_brick], 0)


def neighbourhood(lookup, link_rows, start_row):
    rows = link_rows.shape[0]
    self_rows = start_row + jnp.arange(rows, dtype=jnp.int32)
    complete = jnp.concatenate([link_rows[:, :13], self_rows[:, None], link_rows[:, 13:]], 1)
    complete = jnp.where(complete < 0, lookup.shape[0] - 1, complete)
    bricks = jnp.take(lookup, complete, axis=0)
    channels = bricks.shape[2]
    bricks = bricks.reshape(rows, 3, 3, 3, channels, BS, BS, BS).transpose(0, 4, 1, 5, 2, 6, 3, 7)
    assembled = bricks.reshape(rows, channels, 3 * BS, 3 * BS, 3 * BS)
    return assembled[:, :, BS - 1 : 2 * BS + 1, BS - 1 : 2 * BS + 1, BS - 1 : 2 * BS + 1]


def shifted(padded, k):
    a, b, c = (k // 9, k // 3 % 3, k % 3)
    return padded[:, :, a : a + BS, b : b + BS, c : c + BS].reshape(
        padded.shape[0], padded.shape[1], BS**3
    )


def forward_stack(padded):
    return jnp.stack([shifted(padded, k) for k in range(27)], 1)


def backward_stack(padded):
    return jnp.stack([shifted(padded, 26 - k) for k in range(27)], 1)


def local(
    features, cotangent, first_weight, second_weight, neighbours, send_depth, send_tile, worker_tile
):
    brick_count, channels, cell_count = features.shape
    block_links = neighbours.reshape(-1, brick_block, 26)
    block_starts = jnp.arange(block_links.shape[0], dtype=jnp.int32) * brick_block
    block_shape = (-1, brick_block, channels, cell_count)
    input_lookup = lookup_rows(features, send_depth, send_tile)

    def first_pass(accum, inputs):
        link_rows, start_row = inputs
        pieces = forward_stack(neighbourhood(input_lookup, link_rows, start_row))
        result = jnp.einsum(
            "nkim,kio->nom", pieces, first_weight, preferred_element_type=jnp.float32
        )
        return (accum, result)

    _, pre_act = lax.scan(first_pass, jnp.zeros((), jnp.float32), (block_links, block_starts))
    pre_act = pre_act.reshape(brick_count, channels, cell_count)
    hidden = jax.nn.silu(pre_act).astype(jnp.bfloat16)
    grad_lookup = lookup_rows(cotangent, send_depth, send_tile)

    def second_pass(accum, inputs):
        link_rows, start_row, hidden_rows = inputs
        pieces = backward_stack(neighbourhood(grad_lookup, link_rows, start_row))
        result = jnp.einsum(
            "nkom,kio->nim", pieces, second_weight, preferred_element_type=jnp.float32
        )
        parts = jnp.einsum("nim,nkom->kio", hidden_rows, pieces, preferred_element_type=jnp.float32)
        return (accum + parts, result)

    empty_grad = jnp.zeros((27, channels, channels), jnp.float32)
    second_grad, grad_hidden = lax.scan(
        second_pass, empty_grad, (block_links, block_starts, hidden.reshape(block_shape))
    )
    grad_hidden = grad_hidden.reshape(brick_count, channels, cell_count)
    grad_pre = (grad_hidden * silu_grad(pre_act)).astype(jnp.bfloat16)
    pre_lookup = lookup_rows(grad_pre, send_depth, send_tile)

    def third_pass(accum, inputs):
        link_rows, start_row, input_rows, upstream = inputs
        pieces = backward_stack(neighbourhood(pre_lookup, link_rows, start_row))
        result = upstream.astype(jnp.float32) + jnp.einsum(
            "nkom,kio->nim", pieces, first_weight, preferred_element_type=jnp.float32
        )
        parts = jnp.einsum("nim,nkom->kio", input_rows, pieces, preferred_element_type=jnp.float32)
        return (accum + parts, result.astype(jnp.bfloat16))

    first_grad, grad_input = lax.scan(
        third_pass,
        empty_grad,
        (block_links, block_starts, features.reshape(block_shape), cotangent.reshape(block_shape)),
    )
    grad_input = grad_input.reshape(brick_count, channels, cell_count)
    summed = lax.psum(jnp.stack([first_grad, second_grad]), ("depth", "tile"))
    devices = lax.axis_size("depth") * lax.axis_size("tile")
    factor = float(devices * brick_count * cell_count) ** (-0.5)
    grad_weights = summed * factor
    tiles = lax.axis_size("tile")
    capacity = max(2, 2 * brick_count // tiles)
    destination = worker_tile[:, 0]
    onehot = (destination[:, None] == jnp.arange(tiles, dtype=jnp.int32)[None, :]).astype(jnp.int32)
    before = jnp.cumsum(onehot, axis=0) - onehot
    rank = jnp.sum(before * onehot, 1)
    target = destination * capacity + rank
    outgoing = (
        jnp.zeros((tiles * capacity, channels, cell_count), jnp.bfloat16).at[target].set(grad_input)
    )
    moved_grad = lax.all_to_all(outgoing, "tile", split_axis=0, concat_axis=0, tiled=True)
    return (moved_grad, grad_weights)


def solution(mesh):
    placed = (
        P(("depth", "tile"), None, None),
        P(("depth", "tile"), None, None),
        P(),
        P(),
        P(("depth", "tile"), None),
        P(("depth", "tile"), None, None),
        P(("depth", "tile"), None, None),
        P(("depth", "tile"), None),
    )
    return jax.shard_map(
        local,
        mesh=mesh,
        in_specs=placed,
        out_specs=(P(("depth", "tile"), None, None), P()),
        check_vma=False,
    )
```

profile of v0, /device:TPU:1, one launch (start us, length us, event | category | flops | bytes accessed | tf_op | source)
XLA Modules:
  0.0 797.6 jit_solution(18285770232250657878)
XLA Ops:
  43.1 8.2 %gather_fusion.4 = bf16[216,32,512]{2,1,0:T(8,128)(2,1)} fusion(bf16[17,32,512]{2,1,0:T(8,128)(2,1)S(1)} %constant_dynamic-update-slice_fusion, s32[1024]{0:T(1024)S(1)} %pad_clamp_fusion), kind=kCustom, calls=%fused_computation.2.clone | custom fusion | bytes 14156640 | tf_op jit(solution)/shard_map/while/body/eval_jaxpr/jit(_take)/gather | solution.py:54
  51.4 22.0 %copy.108 = bf16[216,32,512]{1,2,0:T(8,128)(2,1)} copy(bf16[216,32,512]{2,1,0:T(8,128)(2,1)} %gather_fusion.4) | data formatting | bytes 14155776 | tf_op jit(solution)/shard_map/while/body/eval_jaxpr/jit(_take)/gather | solution.py:54
  73.4 8.2 %gather_fusion.9 = bf16[216,32,512]{2,1,0:T(8,128)(2,1)} fusion(bf16[17,32,512]{2,1,0:T(8,128)(2,1)S(1)} %constant_dynamic-update-slice_fusion.33, s32[1024]{0:T(1024)S(1)} %pad_clamp_fusion), kind=kCustom, calls=%fused_computation.13.clone | custom fusion | bytes 14156640 | tf_op jit(solution)/shard_map/while/body/eval_jaxpr/jit(_take)/gather | solution.py:54
  81.6 22.0 %copy.137 = bf16[216,32,512]{1,2,0:T(8,128)(2,1)} copy(bf16[216,32,512]{2,1,0:T(8,128)(2,1)} %gather_fusion.9) | data formatting | bytes 14155776 | tf_op jit(solution)/shard_map/while/body/eval_jaxpr/jit(_take)/gather | solution.py:54
  103.5 37.5 %broadcast_select_fusion = (bf16[8,27,32,512]{2,3,1,0:T(8,128)(2,1)}, bf16[8,27,32,512]{2,3,1,0:T(8,128)(2,1)}) fusion(bf16[8,27,32,512]{2,3,1,0:T(8,128)(2,1)} %bitcast.233, pred[8,27]{1,0:T(8,128)(4,1)S(1)} %get-tuple-element.55, bf16[8,27,32,512]{2,3,1,0:T(8,128)(2,1)} %bitcast.232), kind=kLoop, calls=%fused_computation.16 | loop fusion | flops 7077888 | bytes 28311768 | tf_op jit(solution)/shard_map/while/body/eval_jaxpr/jit(_take)/select_n | solution.py:54
  141.0 19.5 %copy.109 = bf16[8,32,3,8,3,8,3,8]{1,7,6,5,4,3,2,0:T(8,128)(2,1)} copy(bf16[8,32,3,8,3,8,3,8]{1,7,5,3,6,4,2,0:T(8,128)(2,1)} %bitcast.231) | data formatting | bytes 14155776 | tf_op jit(solution)/shard_map/while/body/eval_jaxpr/transpose | solution.py:56
  160.5 8.3 %fusion.17 = (bf16[8,32,8,8,8]{1,4,3,2,0:T(8,128)(2,1)}, bf16[8,32,8,8,8]{1,4,3,2,0:T(8,128)(2,1)}, bf16[8,32,8,8,8]{1,4,3,2,0:T(8,128)(2,1)}, bf16[8,32,8,8,8]{...) fusion(bf16[8,32,24,24,24]{1,4,3,2,0:T(8,128)(2,1)} %bitcast.225), kind=kLoop, calls=%fused_computation.179 | loop fusion | bytes 4194304 | tf_op jit(solution)/shard_map/while/body/eval_jaxpr/slice | solution.py:63
  168.8 19.5 %fusion.16 = (bf16[8,32,8,8,8]{1,4,3,2,0:T(8,128)(2,1)}, bf16[8,32,8,8,8]{1,4,3,2,0:T(8,128)(2,1)}, bf16[8,32,8,8,8]{1,4,3,2,0:T(8,128)(2,1)}, bf16[8,32,8,8,8]{...) fusion(bf16[8,32,24,24,24]{1,4,3,2,0:T(8,128)(2,1)} %bitcast.226), kind=kLoop, calls=%fused_computation.178 | loop fusion | bytes 9961472 | tf_op jit(solution)/shard_map/while/body/eval_jaxpr/slice | solution.py:63
  188.3 19.5 %copy.138 = bf16[8,32,3,8,3,8,3,8]{1,7,6,5,4,3,2,0:T(8,128)(2,1)} copy(bf16[8,32,3,8,3,8,3,8]{1,7,5,3,6,4,2,0:T(8,128)(2,1)} %bitcast.224) | data formatting | bytes 14155776 | tf_op jit(solution)/shard_map/while/body/eval_jaxpr/transpose | solution.py:56
  207.8 9.0 %fusion.15 = (bf16[8,32,8,8,8]{1,4,3,2,0:T(8,128)(2,1)}, bf16[8,32,8,8,8]{1,4,3,2,0:T(8,128)(2,1)}, bf16[8,32,8,8,8]{1,4,3,2,0:T(8,128)(2,1)}, bf16[8,32,8,8,8]{...) fusion(bf16[8,32,24,24,24]{1,4,3,2,0:T(8,128)(2,1)} %bitcast.227), kind=kLoop, calls=%fused_computation.177 | loop fusion | bytes 4194304 | tf_op jit(solution)/shard_map/while/body/eval_jaxpr/slice | solution.py:63
  216.8 18.9 %fusion.14 = (bf16[8,32,8,8,8]{1,4,3,2,0:T(8,128)(2,1)}, bf16[8,32,8,8,8]{1,4,3,2,0:T(8,128)(2,1)S(1)}, bf16[8,32,8,8,8]{1,4,3,2,0:T(8,128)(2,1)S(1)}, bf16[8,32...) fusion(bf16[8,32,24,24,24]{1,4,3,2,0:T(8,128)(2,1)} %bitcast.228), kind=kLoop, calls=%fused_computation.176 | loop fusion | bytes 9961472 | tf_op jit(solution)/shard_map/while/body/eval_jaxpr/slice | solution.py:63
  398.5 4.9 collective-permute-start.8
  407.8 5.6 collective-permute-start.11
  414.3 8.2 %gather_fusion.14 = bf16[216,32,512]{2,1,0:T(8,128)(2,1)} fusion(bf16[17,32,512]{2,1,0:T(8,128)(2,1)S(1)} %constant_dynamic-update-slice_fusion.66, s32[1024]{0:T(1024)S(1)} %pad_clamp_fusion), kind=kCustom, calls=%fused_computation.14.clone | custom fusion | bytes 14156640 | tf_op jit(solution)/shard_map/while/body/eval_jaxpr/jit(_take)/gather | solution.py:54
  422.6 22.0 %copy.167 = bf16[8,27,32,512]{2,3,1,0:T(8,128)(2,1)} copy(bf16[8,27,32,512]{3,2,1,0:T(8,128)(2,1)} %bitcast.235) | data formatting | bytes 14155776 | tf_op jit(solution)/shard_map/while/body/eval_jaxpr/jit(_take)/gather | solution.py:54
  444.5 19.4 %broadcast_select_fusion.2 = bf16[8,27,32,512]{2,3,1,0:T(8,128)(2,1)} fusion(bf16[8,27,32,512]{2,3,1,0:T(8,128)(2,1)} %copy.167, pred[8,27]{1,0:T(8,128)(4,1)S(1)} %get-tuple-element.55), kind=kLoop, calls=%fused_computation.18 | loop fusion | flops 3538944 | bytes 14155992 | tf_op jit(solution)/shard_map/while/body/eval_jaxpr/jit(_take)/select_n | solution.py:54
  463.9 19.7 %copy.168 = bf16[8,32,3,8,3,8,3,8]{1,7,6,5,4,3,2,0:T(8,128)(2,1)} copy(bf16[8,32,3,8,3,8,3,8]{1,7,5,3,6,4,2,0:T(8,128)(2,1)} %bitcast.234) | data formatting | bytes 14155776 | tf_op jit(solution)/shard_map/while/body/eval_jaxpr/transpose | solution.py:56
  483.7 8.6 %fusion.13 = (bf16[8,32,8,8,8]{1,4,3,2,0:T(8,128)(2,1)}, bf16[8,32,8,8,8]{1,4,3,2,0:T(8,128)(2,1)}, bf16[8,32,8,8,8]{1,4,3,2,0:T(8,128)(2,1)}, bf16[8,32,8,8,8]{...) fusion(bf16[8,32,24,24,24]{1,4,3,2,0:T(8,128)(2,1)} %bitcast.229), kind=kLoop, calls=%fused_computation.175 | loop fusion | bytes 4194304 | tf_op jit(solution)/shard_map/while/body/eval_jaxpr/slice | solution.py:63
  492.3 19.9 %fusion.12 = (bf16[8,32,8,8,8]{1,4,3,2,0:T(8,128)(2,1)S(1)}, bf16[8,32,8,8,8]{1,4,3,2,0:T(8,128)(2,1)S(1)}, bf16[8,32,8,8,8]{1,4,3,2,0:T(8,128)(2,1)S(1)}, bf16[...) fusion(bf16[8,32,24,24,24]{1,4,3,2,0:T(8,128)(2,1)} %bitcast.230), kind=kLoop, calls=%fused_computation.174 | loop fusion | bytes 9961472 | tf_op jit(solution)/shard_map/while/body/eval_jaxpr/slice | solution.py:63
  602.7 4.6 fusion.2
  611.0 12.7 %all-to-all-start = ((bf16[64,32,512]{2,1,0:T(8,128)(2,1)}), bf16[64,32,512]{2,1,0:T(8,128)(2,1)S(1)}, u32[]{:S(2)}, u32[]{:S(2)}) async-start(bf16[64,32,512]{2,1,0:T(8,128)(2,1)} %scatter_fusion), calls=%async_computation | async-start | bytes 4194304 | tf_op jit(solution)/shard_map/all_to_all | solution.py:144
  624.0 5.0 convolution_bitcast_fusion.3
  629.0 5.0 convolution_bitcast_fusion.4
  635.0 151.7 %all-reduce.2.cloned.1.call-done = f32[2,27,32,32]{2,3,1,0:T(8,128)} async-done(((f32[2,27,32,32]{2,3,1,0:T(8,128)}), f32[2,27,32,32]{2,3,1,0:T(8,128)}) %all-reduce.2.cloned.1.call-update) | async-done | bytes 221200 | tf_op jit(solution)/shard_map/psum | solution.py:130
  (396 shorter events, 302.2 us)
Async XLA Ops:
  7.2 385.4 %copy-start = (bf16[27,32,32]{2,1,0:T(8,128)(2,1)S(1)}, bf16[27,32,32]{2,1,0:T(8,128)(2,1)}, u32[]{:S(2)}) copy-start(bf16[27,32,32]{2,1,0:T(8,128)(2,1)} %param.17) | copy-start | bytes 165892
  11.1 20.3 %collective-permute-start = (bf16[1,2,32,512]{3,2,1,0:T(8,128)(2,1)S(1)}, bf16[1,2,32,512]{3,2,1,0:T(8,128)(2,1)S(1)}, u32[]{:S(2)}, u32[]{:S(2)}) collective-permute-start(bf16[1,2,32,512]{3,2,1,0:T(8,128)(2,1)S(1)} %get-tuple-element.177), channel_id=1, source_target_pairs={{0,32},{32,64},{64,96},{1,33},{33,65},{65,97},{2,34},{34,66},{66,9... | collective-permute-start | bytes 196616 | tf_op jit(solution)/shard_map/ppermute | solution.py:19
  18.6 12.8 %collective-permute-start.1 = (bf16[1,2,32,512]{3,2,1,0:T(8,128)(2,1)S(1)}, bf16[1,2,32,512]{3,2,1,0:T(8,128)(2,1)S(1)}, u32[]{:S(2)}, u32[]{:S(2)}) collective-permute-start(bf16[1,2,32,512]{3,2,1,0:T(8,128)(2,1)S(1)} %get-tuple-element.175), channel_id=1, source_target_pairs={{32,0},{64,32},{96,64},{33,1},{65,33},{97,65},{34,2},{66,34},{98,6... | collective-permute-start | bytes 196616 | tf_op jit(solution)/shard_map/ppermute | solution.py:20
  19.9 13.0 %collective-permute-start.4 = (bf16[1,2,32,512]{3,2,1,0:T(8,128)(2,1)S(1)}, bf16[1,2,32,512]{3,2,1,0:T(8,128)(2,1)S(1)}, u32[]{:S(2)}, u32[]{:S(2)}) collective-permute-start(bf16[1,2,32,512]{3,2,1,0:T(8,128)(2,1)S(1)} %get-tuple-element.176), channel_id=1, source_target_pairs={{0,32},{32,64},{64,96},{1,33},{33,65},{65,97},{2,34},{34,66},{66,9... | collective-permute-start | bytes 196616 | tf_op jit(solution)/shard_map/ppermute | solution.py:19
  24.1 8.9 %collective-permute-start.5 = (bf16[1,2,32,512]{3,2,1,0:T(8,128)(2,1)S(1)}, bf16[1,2,32,512]{3,2,1,0:T(8,128)(2,1)S(1)}, u32[]{:S(2)}, u32[]{:S(2)}) collective-permute-start(bf16[1,2,32,512]{3,2,1,0:T(8,128)(2,1)S(1)} %get-tuple-element.174), channel_id=1, source_target_pairs={{32,0},{64,32},{96,64},{33,1},{65,33},{97,65},{34,2},{66,34},{98,6... | collective-permute-start | bytes 196616 | tf_op jit(solution)/shard_map/ppermute | solution.py:20
  35.7 6.8 collective-permute-start.2
  38.3 4.3 collective-permute-start.3
  38.4 4.7 collective-permute-start.6
  40.1 33.2 %collective-permute-start.7 = (bf16[1,2,32,512]{3,2,1,0:T(8,128)(2,1)S(1)}, bf16[1,2,32,512]{3,2,1,0:T(8,128)(2,1)S(1)}, u32[]{:S(2)}, u32[]{:S(2)}) collective-permute-start(bf16[1,2,32,512]{3,2,1,0:T(8,128)(2,1)S(1)} %get-tuple-element.170), channel_id=1, source_target_pairs={{1,0},{2,1},{3,2},{4,3},{5,4},{6,5},{7,6},{8,7},{9,8},{10,9},{11,1... | collective-permute-start | bytes 196616 | tf_op jit(solution)/shard_map/ppermute | solution.py:20
  354.1 36.1 %slice-start = ((s8[7077888]{0:T(1024)(128)(4,1)}), s8[2883584]{0:T(1024)(128)(4,1)S(1)}, s32[]{:S(2)}) async-start(s8[7077888]{0:T(1024)(128)(4,1)} %bitcast.236), calls=%async_computation.2 | async-start | bytes 5767168
  356.6 31.4 %copy-start.27 = (bf16[8,1,32,512]{3,2,1,0:T(8,128)(2,1)S(1)}, bf16[8,1,32,512]{3,2,1,0:T(8,128)(2,1)}, u32[]{:S(2)}) copy-start(bf16[8,1,32,512]{3,2,1,0:T(8,128)(2,1)} %copy.134) | copy-start | bytes 786436
  356.6 32.2 %copy-start.24 = (bf16[8,1,32,512]{3,2,1,0:T(8,128)(2,1)S(1)}, bf16[8,1,32,512]{3,2,1,0:T(8,128)(2,1)}, u32[]{:S(2)}) copy-start(bf16[8,1,32,512]{3,2,1,0:T(8,128)(2,1)} %copy.135) | copy-start | bytes 786436
  356.6 32.9 %copy-start.25 = (bf16[8,1,32,512]{3,2,1,0:T(8,128)(2,1)S(1)}, bf16[8,1,32,512]{3,2,1,0:T(8,128)(2,1)}, u32[]{:S(2)}) copy-start(bf16[8,1,32,512]{3,2,1,0:T(8,128)(2,1)} %copy.136) | copy-start | bytes 786436
  356.6 33.6 %copy-start.30 = (bf16[8,1,32,512]{3,2,1,0:T(8,128)(2,1)S(1)}, bf16[8,1,32,512]{3,2,1,0:T(8,128)(2,1)}, u32[]{:S(2)}) copy-start(bf16[8,1,32,512]{3,2,1,0:T(8,128)(2,1)} %copy.140) | copy-start | bytes 786436
  356.6 33.7 %copy-start.31 = (bf16[8,1,32,512]{3,2,1,0:T(8,128)(2,1)S(1)}, bf16[8,1,32,512]{3,2,1,0:T(8,128)(2,1)}, u32[]{:S(2)}) copy-start(bf16[8,1,32,512]{3,2,1,0:T(8,128)(2,1)} %copy.141) | copy-start | bytes 786436
  358.5 31.8 %copy-start.28 = (bf16[8,1,32,512]{3,2,1,0:T(8,128)(2,1)S(1)}, bf16[8,1,32,512]{3,2,1,0:T(8,128)(2,1)}, u32[]{:S(2)}) copy-start(bf16[8,1,32,512]{3,2,1,0:T(8,128)(2,1)} %copy.142) | copy-start | bytes 786436
  397.1 6.3 collective-permute-start.9
  398.5 6.2 collective-permute-start.8
  406.2 7.9 collective-permute-start.10
  407.8 6.5 collective-permute-start.11
  569.7 33.0 %copy-start.1 = (bf16[8,32,512]{2,1,0:T(8,128)(2,1)S(1)}, bf16[8,32,512]{2,1,0:T(8,128)(2,1)}, u32[]{:S(2)}) copy-start(bf16[8,32,512]{2,1,0:T(8,128)(2,1)} %param.15) | copy-start | bytes 786436
  569.7 33.0 %copy-start.51 = (bf16[27,32,32]{2,1,0:T(8,128)(2,1)S(1)}, bf16[27,32,32]{2,1,0:T(8,128)(2,1)}, u32[]{:S(2)}) copy-start(bf16[27,32,32]{2,1,0:T(8,128)(2,1)} %param.16) | copy-start | bytes 165892
  611.0 178.2 %all-to-all-start = ((bf16[64,32,512]{2,1,0:T(8,128)(2,1)}), bf16[64,32,512]{2,1,0:T(8,128)(2,1)S(1)}, u32[]{:S(2)}, u32[]{:S(2)}) async-start(bf16[64,32,512]{2,1,0:T(8,128)(2,1)} %scatter_fusion), calls=%async_computation | async-start | bytes 4194304 | tf_op jit(solution)/shard_map/all_to_all | solution.py:144
  623.7 163.0 %all-reduce.2.cloned.1.call-start = ((), (), s32[]{:S(2)}) async-start(), calls=%async_computation.1 | async-start | bytes 1769472 | tf_op jit(solution)/shard_map/psum | solution.py:130
  (62 other events, 1085.1 us)
Sparse Core Ops, SparseCore 0:
  635.1 151.5 all-reduce.1
where the time goes:
time: 806 us; the launch traced here: 798 us
  local copies, waits for them, and re-layouts  501 us (62%)
  waiting for transfers between devices  154 us (19%)
  other arithmetic  65.6 us (8%)
  starting transfers between devices  44.2 us (5%)
  matrix products  17.3 us (2%)
  between operations  15.6 us (2%)
    psum x1, waiting for transfers between devices, local(): summed = lax.psum(jnp.stack([first_grad, second_grad]), ('depth', 'tile'))  152 us
    reshape x54, local copies, waits for them, and re-layouts, backward_stack(): return jnp.stack([shifted(padded, 26 - k) for k in range(27)], 1)  116 us
    gather x6, local copies, waits for them, and re-layouts, neighbourhood(): bricks = jnp.take(lookup, complete, axis=0)  90.6 us
    slice x6, local copies, waits for them, and re-layouts, shifted(): padded[:, :, a:a + BS, b:b + BS, c:c + BS]  84.2 us
    unnamed x238, local copies, waits for them, and re-layouts  76.7 us
    transpose x3, local copies, waits for them, and re-layouts, neighbourhood(): bricks.reshape(rows, 3, 3, 3, channels, BS, BS, BS)  58.7 us
    select_n x2, other arithmetic, neighbourhood(): bricks = jnp.take(lookup, complete, axis=0)  56.9 us
    reshape x27, local copies, waits for them, and re-layouts, forward_stack(): return jnp.stack([shifted(padded, k) for k in range(27)], 1)  56.8 us
  transfers between devices with their start and end apart: 14, of which 5 were waited for; matrix products, arithmetic and copies ran while one was open for 7% of the time, Pallas kernels for 0%

commit v1 on v0

v1 whole, which is shorter than its diff:
```python
import jax
import jax.numpy as jnp
from jax import lax
from jax.experimental import pallas as pl
from jax.experimental.pallas import tpu as pltpu
from jax.sharding import PartitionSpec as P

F32 = jnp.float32
BF16 = jnp.bfloat16


def iota(shape, dim):
    return lax.broadcasted_iota(jnp.int32, shape, dim)


def tiled_identity(lanes):
    return jnp.where(iota((32, lanes), 1) % 32 == iota((32, lanes), 0), 1.0, 0.0).astype(BF16)


def fill_table(table, slot, brick):
    spread = lax.dot_general(brick, tiled_identity(128), (((0,), (0,)), ((), ())), preferred_element_type=F32)
    table[slot] = spread.reshape(64, 8, 128)


def spread_weight(weight, wide):
    columns = iota((32, 256), 1) // 32
    rows = jnp.dot(weight[...].reshape(864, 32), tiled_identity(256), preferred_element_type=F32).astype(BF16)
    for k in range(27):
        for n in range(8):
            part = jnp.where(columns == n, rows[32 * k : 32 * k + 32], jnp.zeros((), BF16))
            wide[k // 9, pl.ds(256 * (k % 9) + 32 * n, 32), :] = part


def build_shifts(table, links, even, odd):
    lane = iota((8, 128), 1)
    sub = iota((8, 128), 0)

    def one_plane(a_block, a_source, a_row):
        entry = {}
        for rest in range(9):
            k = a_block * 9 + rest
            for n in range(8):
                if k == 13:
                    entry[rest, n] = n
                else:
                    link = links[n, k - (k > 13)]
                    entry[rest, n] = jnp.where(link < 0, 16, link)

        for half in range(2):
            def mixed(rest, b_source):
                parts = [table[entry[rest, 4 * half + j], a_source * 8 + b_source] for j in range(4)]
                low = jnp.where(lane < 32, parts[0], parts[1])
                high = jnp.where(lane < 96, parts[2], parts[3])
                return jnp.where(lane < 64, low, high)

            columns = pl.ds(128 * half, 128)
            rows = []
            for b in range(10):
                b_block, b_source = (b + 7) // 8, (b + 7) % 8
                mid = mixed(b_block * 3 + 1, b_source)
                lower = mixed(b_block * 3, b_source)
                upper = mixed(b_block * 3 + 2, b_source)
                down = pltpu.roll(jnp.where(sub == 7, lower, mid), 1, 0)
                up = pltpu.roll(jnp.where(sub == 0, upper, mid), 7, 0)
                rows.append((down, mid, up))
                if b > 0:
                    for v in range(3):
                        pair = jnp.concatenate([rows[b - 1][v], rows[b][v]], 0).astype(BF16)
                        if b % 2:
                            even[v, a_row, pl.ds(8 * (b - 1), 16), columns] = pair
                        else:
                            odd[v, a_row, pl.ds(8 * (b - 2), 16), columns] = pair

    one_plane(0, 7, 0)

    def middle(a, carry):
        one_plane(1, a, a + 1)
        return carry

    lax.fori_loop(0, 8, middle, 0)
    one_plane(2, 0, 9)


def piece(even, odd, a, rest):
    b, c = rest // 3, rest % 3
    source = odd[c, pl.ds(a, 8)] if b == 1 else even[c, pl.ds(a, 8), pl.ds(8 * b, 64)]
    return source.reshape(512, 256)


def conv_forward(even, odd, wide, total):
    def step(a, carry):
        left = jnp.concatenate([piece(even, odd, a, rest) for rest in range(9)], 1)
        total[...] += jnp.dot(left, wide[a], preferred_element_type=F32)
        return carry

    lax.fori_loop(0, 3, step, 0)


def conv_backward(even, odd, wide, total):
    def step(a, carry):
        acc = total[...]
        for rest in range(9):
            acc += lax.dot_general(
                piece(even, odd, a, rest), wide[2 - a, pl.ds(256 * (8 - rest), 256), :], (((1,), (1,)), ((), ())), preferred_element_type=F32
            )
        total[...] = acc
        return carry

    lax.fori_loop(0, 3, step, 0)


def weight_gradient(left_of, even, odd, folded):
    lane = iota((32, 128), 1)

    def step(a, carry):
        for rest in range(9):
            full = jnp.dot(left_of(), piece(even, odd, a, rest), preferred_element_type=F32)
            halves = []
            for half in range(2):
                parts = [full[128 * half + 32 * j : 128 * half + 32 * j + 32, 128 * half : 128 * half + 128] for j in range(4)]
                low = jnp.where(lane < 32, parts[0], parts[1])
                high = jnp.where(lane < 96, parts[2], parts[3])
                halves.append(jnp.where(lane < 64, low, high))
            both = halves[0] + halves[1]
            both = both + pltpu.roll(both, 64, 1)
            both = both + pltpu.roll(both, 32, 1)
            folded[pl.ds(pl.multiple_of(32 * (9 * (2 - a) + 8 - rest), 32), 32), :] = both
        return carry

    lax.fori_loop(0, 3, step, 0)


def pack_gradient(folded, packed):
    lane = iota((8, 128), 1)
    for r in range(27):
        parts = [folded[pl.ds(8 * (27 * g + r), 8), :] for g in range(4)]
        low = jnp.where(lane < 32, parts[0], parts[1])
        high = jnp.where(lane < 96, parts[2], parts[3])
        packed[r] = jnp.where(lane < 64, low, high)
    packed[27:32] = jnp.zeros((5, 8, 128), F32)

MESH = pl.DeviceIdType.MESH
DEPTHS, TILES = 4, 32


def remote(source, target, send, receive, device):
    return pltpu.make_async_remote_copy(
        src_ref=source, dst_ref=target, send_sem=send, recv_sem=receive, device_id=device, device_id_type=MESH
    )


def place():
    d, t = lax.axis_index("depth"), lax.axis_index("tile")
    return d, t, (t // 2) * 2, t % 2


def greet():
    d, t, chip, core = place()
    barrier = pltpu.get_barrier_semaphore()

    def tile_peer(i, carry):
        pl.semaphore_signal(barrier, inc=1, device_id=(d, (t + i) % TILES), device_id_type=MESH)
        return carry

    def depth_peer(i, carry):
        other = ((d + 1 + i // 2) % DEPTHS, chip + i % 2)
        pl.semaphore_signal(barrier, inc=1, device_id=other, device_id_type=MESH)
        return carry

    lax.fori_loop(1, TILES, tile_peer, 0)
    lax.fori_loop(0, 2 * (DEPTHS - 1), depth_peer, 0)
    return barrier


def depth_copies(stage, land, sends, receives):
    d, t, _, _ = place()
    return (
        remote(stage.at[0], land.at[1], sends.at[0], receives.at[1], ((d + DEPTHS - 1) % DEPTHS, t)),
        remote(stage.at[1], land.at[0], sends.at[1], receives.at[0], ((d + 1) % DEPTHS, t)),
    )


def tile_copies(stage, land, sends, receives):
    d, t, _, _ = place()
    return (
        remote(stage.at[0], land.at[1], sends.at[0], receives.at[1], (d, (t + TILES - 1) % TILES)),
        remote(stage.at[1], land.at[0], sends.at[1], receives.at[0], (d, (t + 1) % TILES)),
    )


def stage_depth(fields, send_depth, stage):
    for side in range(2):
        for f, field in enumerate(fields):
            for j in range(2):
                stage[side, 2 * f + j] = field[send_depth[0, side, j]]


def accept_depth(fields, land, sections, tables):
    d, _, _, _ = place()
    inner = (d > 0, d < DEPTHS - 1)
    for f, field in enumerate(fields):
        sections[f, 0:8] = field[...]
        for side in range(2):
            for j in range(2):
                value = land[side, 2 * f + j]
                value = jnp.where(inner[side], value, jnp.zeros_like(value))
                sections[f, 8 + 2 * side + j] = value


def stage_tile(count, sections, send_tile, stage):
    for side in range(2):
        for f in range(count):
            for j in range(2):
                stage[side, 2 * f + j] = sections[f, send_tile[0, side, j]]


def table_own(fields, tables):
    for field, table in zip(fields, tables):
        for m in range(8):
            fill_table(table, m, field[m])


def table_depth(sections, tables):
    for f, table in enumerate(tables):
        for j in range(4):
            fill_table(table, 8 + j, sections[f, 8 + j])


def table_tile(land, tables):
    for f, table in enumerate(tables):
        for side in range(2):
            for j in range(2):
                fill_table(table, 12 + 2 * side + j, land[side, 2 * f + j])


def ring_copy(i, source, target, sends, receives, group):
    d, t, chip, core = place()
    if group == 8:
        me = d * 2 + core
        peer = (me + i) % 8
        device = (peer // 2, chip + peer % 2)
    elif group == 16:
        me = t // 2
        peer = (me + i) % 16
        device = (d, 2 * peer + core)
    else:
        me = t
        peer = (t + i) % TILES
        device = (d, peer)
    return remote(source(me, peer), target(me, peer), sends.at[peer], receives.at[me], device)


def arrived_copy(i, source, target, sends, receives, group):
    d, t, chip, core = place()
    if group == 8:
        me = d * 2 + core
        peer = (me + i) % 8
        device = (peer // 2, chip + peer % 2)
    elif group == 16:
        me = t // 2
        peer = (me + i) % 16
        device = (d, 2 * peer + core)
    else:
        me = t
        peer = (t + i) % TILES
        device = (d, peer)
    return remote(source(me, peer), target(peer, me), sends.at[peer], receives.at[peer], device)


def start_all(*args):
    def step(i, carry):
        ring_copy(i, *args).start()
        return carry

    lax.fori_loop(1, args[-1], step, 0)


def wait_arrived(*args):
    def step(i, carry):
        arrived_copy(i, *args).wait_recv()
        return carry

    lax.fori_loop(1, args[-1], step, 0)


def wait_sent(*args):
    def step(i, carry):
        ring_copy(i, *args).wait_send()
        return carry

    lax.fori_loop(1, args[-1], step, 0)


def reduce_plans(packed, land_a, part, land_b, result, sems):
    a_send, a_receive, b_send, b_receive, c_send, c_receive = sems
    first = (lambda me, peer: packed.at[pl.ds(4 * peer, 4)], lambda me, peer: land_a.at[me], a_send, a_receive, 8)
    second = (lambda me, peer: part, lambda me, peer: land_b.at[me], b_send, b_receive, 16)
    third = (lambda me, peer: land_b.at[16], lambda me, peer: result.at[pl.ds(4 * me, 4)], c_send, c_receive, 8)
    return first, second, third


def reduce_first(plans, packed, land_a, part, land_b):
    d, t, chip, core = place()
    me = d * 2 + core
    wait_arrived(*plans[0])
    land_a[me] = packed[pl.ds(4 * me, 4)]
    total = land_a[0]
    for j in range(1, 8):
        total += land_a[j]
    part[...] = total
    land_b[t // 2] = total
    start_all(*plans[1])


def reduce_second(plans, part, land_b, result, factor):
    d, t, chip, core = place()
    me = d * 2 + core
    wait_arrived(*plans[1])
    total = land_b[0]
    for j in range(1, 16):
        total += land_b[j]
    total = total * factor
    land_b[16] = total
    result[pl.ds(4 * me, 4)] = total
    start_all(*plans[2])


def unpack_gradient(result, out, w):
    for r in range(27):
        tile = result[r]
        for g in range(4):
            t = 27 * g + r
            moved = tile if g == 0 else pltpu.roll(tile, 128 - 32 * g, 1)
            out[w, t // 4, pl.ds(8 * (t % 4), 8), :] = moved[:, :32]


def kernel(
    features, cotangent, first_weight, second_weight, links, send_depth, send_tile, workers,
    moved, gradients,
    table_x, table_g, even_x, odd_x, even_g, odd_g, wide_first, wide_second, pre, back, hidden, folded,
    grad_pre, grad_input, outgoing,
    stage_d, land_d, stage_t, land_t, sections,
    stage_d2, land_d2, stage_t2, land_t2, sections2,
    packed, land_a, part, land_b, result,
    d_send, d_receive, t_send, t_receive, d2_send, d2_receive, t2_send, t2_receive,
    m_send, m_receive, own_sem, a_send, a_receive, b_send, b_receive, c_send, c_receive,
):
    d, t, chip, core = place()
    fields, tables = (features, cotangent), (table_x, table_g)
    barrier = greet()
    stage_depth(fields, send_depth, stage_d)
    pl.semaphore_wait(barrier, TILES - 1 + 2 * (DEPTHS - 1))
    along_depth = depth_copies(stage_d, land_d, d_send, d_receive)
    for copy in along_depth:
        copy.start()
    table_own(fields, tables)
    table_x[16] = jnp.zeros((64, 8, 128), F32)
    table_g[16] = jnp.zeros((64, 8, 128), F32)
    for copy in along_depth:
        copy.wait()
    accept_depth(fields, land_d, sections, tables)
    stage_tile(2, sections, send_tile, stage_t)
    along_tile = tile_copies(stage_t, land_t, t_send, t_receive)
    for copy in along_tile:
        copy.start()
    table_depth(sections, tables)
    spread_weight(first_weight, wide_first)
    spread_weight(second_weight, wide_second)
    for copy in along_tile:
        copy.wait()
    table_tile(land_t, tables)
    build_shifts(table_x, links, even_x, odd_x)
    build_shifts(table_g, links, even_g, odd_g)
    pre[...] = jnp.zeros((512, 256), F32)
    back[...] = jnp.zeros((512, 256), F32)
    conv_forward(even_x, odd_x, wide_first, pre)
    conv_backward(even_g, odd_g, wide_second, back)
    value = pre[...]
    sigma = 1.0 / (1.0 + jnp.exp(-value))
    hidden[...] = (value * sigma).T.astype(BF16)
    grad_pre[...] = (back[...] * sigma * (1.0 + value * (1.0 - sigma))).T.astype(BF16).reshape(8, 32, 512)

    stage_depth((grad_pre,), send_depth, stage_d2)
    along_depth = depth_copies(stage_d2, land_d2, d2_send, d2_receive)
    for copy in along_depth:
        copy.start()
    weight_gradient(lambda: hidden[...], even_g, odd_g, folded)
    for copy in along_depth:
        copy.wait()
    accept_depth((grad_pre,), land_d2, sections2, tables)
    stage_tile(1, sections2, send_tile, stage_t2)
    along_tile = tile_copies(stage_t2, land_t2, t2_send, t2_receive)
    for copy in along_tile:
        copy.start()
    pack_gradient(folded, packed.at[1])
    plans = [
        reduce_plans(
            packed.at[w], land_a.at[w], part.at[w], land_b.at[w], result.at[w],
            tuple(s.at[w] for s in (a_send, a_receive, b_send, b_receive, c_send, c_receive)),
        )
        for w in range(2)
    ]
    start_all(*plans[1][0])
    table_own((grad_pre,), tables[:1])
    table_depth(sections2, tables[:1])
    for copy in along_tile:
        copy.wait()
    table_tile(land_t2, tables[:1])
    build_shifts(table_x, links, even_x, odd_x)
    back[...] = jnp.zeros((512, 256), F32)
    conv_backward(even_x, odd_x, wide_first, back)
    grad_input[0:8] = (back[...].T.reshape(8, 32, 512) + cotangent[...].astype(F32)).astype(BF16)
    grad_input[8] = jnp.zeros((32, 512), BF16)

    names = [workers[n, 0] for n in range(8)]
    slots = []
    for n in range(8):
        rank = jnp.int32(0)
        for m in range(n):
            rank = rank + jnp.where(names[m] == names[n], 1, 0)
        slots.append(2 * names[n] + rank)

    def place_brick(s, carry):
        brick = jnp.int32(8)
        for n in range(8):
            brick = jnp.where(slots[n] == s, n, brick)
        outgoing[s] = grad_input[brick]
        return carry

    lax.fori_loop(0, 2 * TILES, place_brick, 0)
    own = pltpu.make_async_copy(outgoing.at[pl.ds(2 * t, 2)], moved.at[pl.ds(2 * t, 2)], own_sem)
    own.start()
    moves = (
        lambda me, peer: outgoing.at[pl.ds(2 * peer, 2)],
        lambda me, peer: moved.at[pl.ds(2 * me, 2)],
        m_send, m_receive, TILES,
    )
    start_all(*moves)

    factor = float(DEPTHS * TILES * 8 * 512) ** (-0.5)
    reduce_first(plans[1], packed.at[1], land_a.at[1], part.at[1], land_b.at[1])
    weight_gradient(lambda: features[...].reshape(256, 512), even_x, odd_x, folded)
    pack_gradient(folded, packed.at[0])
    start_all(*plans[0][0])
    reduce_second(plans[1], part.at[1], land_b.at[1], result.at[1], factor)
    reduce_first(plans[0], packed.at[0], land_a.at[0], part.at[0], land_b.at[0])
    wait_arrived(*plans[1][2])
    unpack_gradient(result.at[1], gradients, 1)
    reduce_second(plans[0], part.at[0], land_b.at[0], result.at[0], factor)
    wait_arrived(*plans[0][2])
    unpack_gradient(result.at[0], gradients, 0)
    for w in range(2):
        for plan in plans[w]:
            wait_sent(*plan)
    own.wait()
    wait_arrived(*moves)
    wait_sent(*moves)


def local(features, cotangent, first_weight, second_weight, neighbours, send_depth, send_tile, worker_tile):
    vmem, smem = pl.BlockSpec(memory_space=pltpu.VMEM), pl.BlockSpec(memory_space=pltpu.SMEM)
    brick = (32, 512)
    shifts = [pltpu.VMEM((3, 10, 80, 256), BF16), pltpu.VMEM((3, 10, 64, 256), BF16)]

    def halo(count):
        return [pltpu.VMEM((2, 2 * count, *brick), BF16)] * 4 + [pltpu.VMEM((count, 12, *brick), BF16)]

    dma = pltpu.SemaphoreType.DMA
    return pl.pallas_call(
        kernel,
        out_shape=(
            jax.ShapeDtypeStruct((2 * TILES, *brick), BF16),
            jax.ShapeDtypeStruct((2, 27, 32, 32), F32),
        ),
        in_specs=[vmem] * 4 + [smem] * 4,
        out_specs=(pl.BlockSpec(memory_space=pl.ANY), vmem),
        scratch_shapes=[pltpu.VMEM((17, 64, 8, 128), F32)] * 2
        + shifts * 2
        + [pltpu.VMEM((3, 2304, 256), BF16)] * 2
        + [pltpu.VMEM((512, 256), F32)] * 2
        + [pltpu.VMEM((256, 512), BF16), pltpu.VMEM((864, 128), F32)]
        + [pltpu.VMEM((8, *brick), BF16), pltpu.VMEM((9, *brick), BF16), pltpu.VMEM((64, *brick), BF16)]
        + halo(2)
        + halo(1)
        + [
            pltpu.VMEM((2, 32, 8, 128), F32),
            pltpu.VMEM((2, 8, 4, 8, 128), F32),
            pltpu.VMEM((2, 4, 8, 128), F32),
            pltpu.VMEM((2, 17, 4, 8, 128), F32),
            pltpu.VMEM((2, 32, 8, 128), F32),
        ]
        + [dma((2,))] * 8
        + [dma((TILES,))] * 2
        + [dma]
        + [dma((2, 8))] * 2
        + [dma((2, 16))] * 2
        + [dma((2, 8))] * 2,
        compiler_params=pltpu.CompilerParams(
            collective_id=0, has_side_effects=True, vmem_limit_bytes=50 * 2**20
        ),
    )(features, cotangent, first_weight, second_weight, neighbours, send_depth, send_tile, worker_tile)


def solution(mesh):
    rows = P(("depth", "tile"))
    placed = (rows, rows, P(), P(), rows, rows, rows, rows)
    return jax.shard_map(local, mesh=mesh, in_specs=placed, out_specs=(rows, P()), check_vma=False)
```

time: 806 us -> 98.1 us (0.12)
  local copies, waits for them, and re-layouts: 501 us -> 8.78 us
  waiting for transfers between devices: 154 us -> 0 us
  Pallas kernels: 0 us -> 88.3 us
  other arithmetic: 65.6 us -> 0 us
  starting transfers between devices: 44.2 us -> 0 us
  matrix products: 17.3 us -> 0 us
  between operations: 15.6 us -> 0.65 us
    reshape x81 -> x0, local copies, waits for them, and re-layouts: 173 us -> none  [the longest x54 116 us: backward_stack(): return jnp.stack([shifted(padded, 26 - k) for k in range(27)], 1)]
    psum x1 -> x0, waiting for transfers between devices: 152 us -> none  [local(): summed = lax.psum(jnp.stack([first_grad, second_grad]), ('depth', 'tile'))]
    gather x18 -> x0, local copies, waits for them, and re-layouts: 101 us -> none  [the longest x6 90.6 us: neighbourhood(): bricks = jnp.take(lookup, complete, axis=0)]
    pallas_call x0 -> x1, Pallas kernels: none -> 88.3 us  [local(): pl.pallas_call(kernel, out_shape=(jax.ShapeDtypeStruct((2 * TILES, *brick...]
    slice x7 -> x0, local copies, waits for them, and re-layouts: 85 us -> none  [the longest x6 84.2 us: shifted(): padded[:, :, a:a + BS, b:b + BS, c:c + BS]]
    unnamed x238 -> x17, local copies, waits for them, and re-layouts: 76.7 us -> 8.78 us
    transpose x3 -> x0, local copies, waits for them, and re-layouts: 58.7 us -> none  [neighbourhood(): bricks.reshape(rows, 3, 3, 3, channels, BS, BS, BS)]
    select_n x3 -> x0, other arithmetic: 56.9 us -> none  [the longest x2 56.9 us: neighbourhood(): bricks = jnp.take(lookup, complete, axis=0)]
  transfers between devices with their start and end apart: 14 -> 0, of which waited for: 5 -> 0; matrix products, arithmetic and copies ran while one was open for 7% -> 0% of each run, Pallas kernels for 0% -> 0%
where the time goes in v1:
time: 98.1 us; the launch traced here: 97.8 us
  Pallas kernels  88.3 us (90%)
  local copies, waits for them, and re-layouts  8.78 us (9%)
    pallas_call x1, Pallas kernels, local(): pl.pallas_call(kernel, out_shape=(jax.ShapeDtypeStruct((2 * TILES, *brick...  88.3 us
    unnamed x17, local copies, waits for them, and re-layouts  8.78 us

profile of v1, /device:TPU:1, one launch (start us, length us, event | category | flops | bytes accessed | tf_op | source)
XLA Modules:
  0.0 97.8 jit_solution(5524296213461306000)
XLA Ops:
  0.6 0.7 copy.10.workers
  1.4 0.0 copy-start
  1.4 0.9 copy-done
  2.3 0.0 copy-start.1
  2.3 0.9 copy-done.1
  3.3 0.0 copy-start.2
  3.3 0.9 copy-done.2
  4.2 0.0 copy-start.3
  4.2 0.9 copy-done.3
  5.1 0.0 copy-start.4
  5.1 0.7 copy-done.4
  5.8 0.0 copy-start.5
  5.8 0.7 copy-done.5
  6.5 0.0 copy-start.6
  6.5 0.7 copy-done.6
  7.2 88.3 %shard_map.95 = (bf16[64,32,512]{2,1,0:T(8,128)(2,1)S(1)}, f32[2,27,32,32]{3,2,1,0:T(8,128)S(1)}) custom-call(bf16[8,32,512]{2,1,0:T(8,128)(2,1)S(1)} %copy-done, bf16[8,32,512]{2,1,0:T(8,128)(2,1)S(1)} %copy-done.1, bf16[27,32,32]{2,1,0:T(8,128)(2,1)S(1)} %copy-done.2, bf16[27,32,32]{2,1,0:T(8,128)(2,1)S(1)} %copy-done.3, s32[8,26]{1,0:T(8,128)S(1)} %copy-done.4, ...), custom_call_target="tpu_custom_call" | custom-call | tf_op jit(solution)/shard_map/pallas_call | solution.py:469
  95.5 1.3 %copy.13 = bf16[64,32,512]{2,1,0:T(8,128)(2,1)} copy(bf16[64,32,512]{2,1,0:T(8,128)(2,1)S(1)} %get-tuple-element.4) | data formatting | bytes 4194304
  96.9 0.9 copy.14
Async XLA Ops:
  1.4 0.9 copy-start
  2.3 0.9 copy-start.1
  3.3 0.9 copy-start.2
  4.2 0.9 copy-start.3
  5.1 0.7 copy-start.4
  5.8 0.7 copy-start.5
  6.5 0.7 copy-start.6

commit v2 on v1

--- a/solution.py
+++ b/solution.py
@@ -233,6 +233,35 @@
                 fill_table(table, 12 + 2 * side + j, land[side, 2 * f + j])
 
 
+ORDER = (
+    (1, 2, 1), (3, 1, 0), (0, 3, 1), (2, 2, 0), (0, 0, 1), (1, 3, 0),
+    (3, 1, 1), (1, 0, 0), (2, 2, 1), (0, 1, 0), (1, 3, 1), (3, 2, 0),
+    (1, 0, 1), (2, 3, 0), (0, 1, 1), (2, 0, 0), (3, 2, 1), (1, 1, 0),
+    (2, 3, 1), (0, 2, 0), (2, 0, 1), (3, 3, 0), (1, 1, 1), (3, 0, 0),
+    (0, 2, 1), (2, 1, 0), (3, 3, 1), (1, 2, 0), (3, 0, 1), (0, 3, 0),
+    (2, 1, 1),
+)
+
+
+def shifted_tile(i, sign):
+    t = lax.axis_index("tile")
+    dy, dx, dc = ORDER[i]
+    y, x, core = t // 8, (t // 2) % 4, t % 2
+    return ((y + sign * dy + 4) % 4) * 8 + ((x + sign * dx + 4) % 4) * 2 + (core + dc) % 2
+
+
+def move(i, outgoing, moved, sends, receives):
+    d, t = lax.axis_index("depth"), lax.axis_index("tile")
+    peer = shifted_tile(i, 1)
+    return remote(outgoing.at[pl.ds(2 * peer, 2)], moved.at[pl.ds(2 * t, 2)], sends.at[i], receives.at[i], (d, peer))
+
+
+def landed(i, outgoing, moved, sends, receives):
+    d = lax.axis_index("depth")
+    peer = shifted_tile(i, -1)
+    return remote(outgoing.at[pl.ds(2 * peer, 2)], moved.at[pl.ds(2 * peer, 2)], sends.at[i], receives.at[i], (d, peer))
+
+
 def ring_copy(i, source, target, sends, receives, group):
     d, t, chip, core = place()
     if group == 8:
@@ -335,19 +364,29 @@
 
 
 def kernel(
-    features, cotangent, first_weight, second_weight, links, send_depth, send_tile, workers,
-    moved, gradients,
+    features_in, cotangent_in, first_in, second_in, links_in, depth_in, tile_in, workers_in,
+    moved, gradients_out,
+    features, cotangent, first_weight, second_weight, links, send_depth, send_tile, workers, gradients,
     table_x, table_g, even_x, odd_x, even_g, odd_g, wide_first, wide_second, pre, back, hidden, folded,
     grad_pre, grad_input, outgoing,
     stage_d, land_d, stage_t, land_t, sections,
     stage_d2, land_d2, stage_t2, land_t2, sections2,
     packed, land_a, part, land_b, result,
     d_send, d_receive, t_send, t_receive, d2_send, d2_receive, t2_send, t2_receive,
-    m_send, m_receive, own_sem, a_send, a_receive, b_send, b_receive, c_send, c_receive,
+    load_sem, store_sem, m_send, m_receive, own_sem, a_send, a_receive, b_send, b_receive, c_send, c_receive,
 ):
     d, t, chip, core = place()
     fields, tables = (features, cotangent), (table_x, table_g)
+    pairs = (
+        (features_in, features), (cotangent_in, cotangent), (depth_in, send_depth), (tile_in, send_tile),
+        (links_in, links), (workers_in, workers), (first_in, first_weight), (second_in, second_weight),
+    )
+    loads = [pltpu.make_async_copy(source, target, load_sem.at[i]) for i, (source, target) in enumerate(pairs)]
+    for load in loads:
+        load.start()
     barrier = greet()
+    for load in loads:
+        load.wait()
     stage_depth(fields, send_depth, stage_d)
     pl.semaphore_wait(barrier, TILES - 1 + 2 * (DEPTHS - 1))
     along_depth = depth_copies(stage_d, land_d, d_send, d_receive)
@@ -356,6 +395,7 @@
     table_own(fields, tables)
     table_x[16] = jnp.zeros((64, 8, 128), F32)
     table_g[16] = jnp.zeros((64, 8, 128), F32)
+    spread_weight(first_weight, wide_first)
     for copy in along_depth:
         copy.wait()
     accept_depth(fields, land_d, sections, tables)
@@ -364,7 +404,6 @@
     for copy in along_tile:
         copy.start()
     table_depth(sections, tables)
-    spread_weight(first_weight, wide_first)
     spread_weight(second_weight, wide_second)
     for copy in along_tile:
         copy.wait()
@@ -409,10 +448,11 @@
     build_shifts(table_x, links, even_x, odd_x)
     back[...] = jnp.zeros((512, 256), F32)
     conv_backward(even_x, odd_x, wide_first, back)
+    reduce_first(plans[1], packed.at[1], land_a.at[1], part.at[1], land_b.at[1])
     grad_input[0:8] = (back[...].T.reshape(8, 32, 512) + cotangent[...].astype(F32)).astype(BF16)
     grad_input[8] = jnp.zeros((32, 512), BF16)
 
-    names = [workers[n, 0] for n in range(8)]
+    names = [workers[0, n] for n in range(8)]
     slots = []
     for n in range(8):
         rank = jnp.int32(0)
@@ -430,35 +470,53 @@
     lax.fori_loop(0, 2 * TILES, place_brick, 0)
     own = pltpu.make_async_copy(outgoing.at[pl.ds(2 * t, 2)], moved.at[pl.ds(2 * t, 2)], own_sem)
     own.start()
-    moves = (
-        lambda me, peer: outgoing.at[pl.ds(2 * peer, 2)],
-        lambda me, peer: moved.at[pl.ds(2 * me, 2)],
-        m_send, m_receive, TILES,
-    )
-    start_all(*moves)
-
     factor = float(DEPTHS * TILES * 8 * 512) ** (-0.5)
-    reduce_first(plans[1], packed.at[1], land_a.at[1], part.at[1], land_b.at[1])
+    for i in range(0, 10):
+        move(i, outgoing, moved, m_send, m_receive).start()
     weight_gradient(lambda: features[...].reshape(256, 512), even_x, odd_x, folded)
     pack_gradient(folded, packed.at[0])
     start_all(*plans[0][0])
+    for i in range(10, 17):
+        move(i, outgoing, moved, m_send, m_receive).start()
     reduce_second(plans[1], part.at[1], land_b.at[1], result.at[1], factor)
     reduce_first(plans[0], packed.at[0], land_a.at[0], part.at[0], land_b.at[0])
+    for i in range(17, 24):
+        move(i, outgoing, moved, m_send, m_receive).start()
     wait_arrived(*plans[1][2])
     unpack_gradient(result.at[1], gradients, 1)
     reduce_second(plans[0], part.at[0], land_b.at[0], result.at[0], factor)
+    for i in range(24, 31):
+        move(i, outgoing, moved, m_send, m_receive).start()
     wait_arrived(*plans[0][2])
     unpack_gradient(result.at[0], gradients, 0)
+    store = pltpu.make_async_copy(gradients, gradients_out, store_sem)
+    store.start()
     for w in range(2):
         for plan in plans[w]:
             wait_sent(*plan)
     own.wait()
-    wait_arrived(*moves)
-    wait_sent(*moves)
+    for i in range(31):
+        landed(i, outgoing, moved, m_send, m_receive).wait_recv()
+        move(i, outgoing, moved, m_send, m_receive).wait_send()
+    store.wait()
+
+
+def hand_over(moved_in, gradients_in, moved, gradients, held, held_gradients, in_sems, out_sems):
+    spans = [(moved_in, held, moved, pl.ds(8 * i, 8)) for i in range(8)]
+    spans += [(gradients_in, held_gradients, gradients, pl.ds(i, 1)) for i in range(2)]
+    loads = [pltpu.make_async_copy(a.at[at], b.at[at], in_sems.at[i]) for i, (a, b, c, at) in enumerate(spans)]
+    stores = [pltpu.make_async_copy(b.at[at], c.at[at], out_sems.at[i]) for i, (a, b, c, at) in enumerate(spans)]
+    for load in loads:
+        load.start()
+    for load, store in zip(loads, stores):
+        load.wait()
+        store.start()
+    for store in stores:
+        store.wait()
 
 
 def local(features, cotangent, first_weight, second_weight, neighbours, send_depth, send_tile, worker_tile):
-    vmem, smem = pl.BlockSpec(memory_space=pltpu.VMEM), pl.BlockSpec(memory_space=pltpu.SMEM)
+    anywhere = pl.BlockSpec(memory_space=pl.ANY)
     brick = (32, 512)
     shifts = [pltpu.VMEM((3, 10, 80, 256), BF16), pltpu.VMEM((3, 10, 64, 256), BF16)]
 
@@ -466,15 +524,19 @@
         return [pltpu.VMEM((2, 2 * count, *brick), BF16)] * 4 + [pltpu.VMEM((count, 12, *brick), BF16)]
 
     dma = pltpu.SemaphoreType.DMA
-    return pl.pallas_call(
+    results = pl.pallas_call(
         kernel,
         out_shape=(
             jax.ShapeDtypeStruct((2 * TILES, *brick), BF16),
             jax.ShapeDtypeStruct((2, 27, 32, 32), F32),
         ),
-        in_specs=[vmem] * 4 + [smem] * 4,
-        out_specs=(pl.BlockSpec(memory_space=pl.ANY), vmem),
-        scratch_shapes=[pltpu.VMEM((17, 64, 8, 128), F32)] * 2
+        in_specs=[anywhere] * 8,
+        out_specs=(anywhere, anywhere),
+        scratch_shapes=[pltpu.VMEM((8, *brick), BF16)] * 2
+        + [pltpu.VMEM((27, 32, 32), BF16)] * 2
+        + [pltpu.SMEM((8, 26), jnp.int32), pltpu.SMEM((1, 2, 2), jnp.int32), pltpu.SMEM((1, 2, 2), jnp.int32), pltpu.SMEM((1, 8), jnp.int32)]
+        + [pltpu.VMEM((2, 27, 32, 32), F32)]
+        + [pltpu.VMEM((17, 64, 8, 128), F32)] * 2
         + shifts * 2
         + [pltpu.VMEM((3, 2304, 256), BF16)] * 2
         + [pltpu.VMEM((512, 256), F32)] * 2
@@ -490,15 +552,24 @@
             pltpu.VMEM((2, 32, 8, 128), F32),
         ]
         + [dma((2,))] * 8
-        + [dma((TILES,))] * 2
+        + [dma((8,)), dma]
+        + [dma((TILES - 1,))] * 2
         + [dma]
         + [dma((2, 8))] * 2
         + [dma((2, 16))] * 2
         + [dma((2, 8))] * 2,
         compiler_params=pltpu.CompilerParams(
-            collective_id=0, has_side_effects=True, vmem_limit_bytes=50 * 2**20
+            collective_id=0, has_side_effects=True, vmem_limit_bytes=64 * 2**20 - 2**17
         ),
-    )(features, cotangent, first_weight, second_weight, neighbours, send_depth, send_tile, worker_tile)
+    )(features, cotangent, first_weight, second_weight, neighbours, send_depth, send_tile, worker_tile.reshape(1, 8))
+    return pl.pallas_call(
+        hand_over,
+        out_shape=tuple(jax.ShapeDtypeStruct(r.shape, r.dtype) for r in results),
+        in_specs=[anywhere] * 2,
+        out_specs=(anywhere, anywhere),
+        scratch_shapes=[pltpu.VMEM((2 * TILES, *brick), BF16), pltpu.VMEM((2, 27, 32, 32), F32), dma((10,)), dma((10,))],
+        compiler_params=pltpu.CompilerParams(vmem_limit_bytes=64 * 2**20 - 2**17),
+    )(*results)
 
 
 def solution(mesh):

time: 98.1 us -> 75.5 us (0.77)
  Pallas kernels: 88.3 us -> 74.7 us
  local copies, waits for them, and re-layouts: 8.78 us -> 0 us
    pallas_call x1, Pallas kernels: 88.3 us -> 72 us  [local(): pl.pallas_call(kernel, out_shape=(jax.ShapeDtypeStruct((2 * TILES, *brick...]
    unnamed x17 -> x0, local copies, waits for them, and re-layouts: 8.78 us -> none
    pallas_call x0 -> x1, Pallas kernels: none -> 2.73 us  [local(): pl.pallas_call(hand_over, out_shape=tuple((jax.ShapeDtypeStruct(r.shape,...]
where the time goes in v2:
time: 75.5 us; the launch traced here: 75.3 us
  Pallas kernels  74.7 us (99%)
    pallas_call x1, Pallas kernels, local(): pl.pallas_call(kernel, out_shape=(jax.ShapeDtypeStruct((2 * TILES, *brick...  72 us
    pallas_call x1, Pallas kernels, local(): pl.pallas_call(hand_over, out_shape=tuple((jax.ShapeDtypeStruct(r.shape,...  2.73 us

profile of v2, /device:TPU:1, one launch (start us, length us, event | category | flops | bytes accessed | tf_op | source)
XLA Modules:
  0.0 75.3 jit_solution(18088190744248901002)
XLA Ops:
  0.6 72.0 %shard_map.95 = (bf16[64,32,512]{2,1,0:T(8,128)(2,1)}, f32[2,27,32,32]{3,2,1,0:T(8,128)}) custom-call(bf16[8,32,512]{2,1,0:T(8,128)(2,1)} %features_in.1, bf16[8,32,512]{2,1,0:T(8,128)(2,1)} %cotangent_in.1, bf16[27,32,32]{2,1,0:T(8,128)(2,1)} %first_in.1, bf16[27,32,32]{2,1,0:T(8,128)(2,1)} %second_in.1, s32[8,26]{1,0:T(8,128)} %links_in.1, ...), custom_call_target="tpu_custom_call" | custom-call | tf_op jit(solution)/shard_map/pallas_call | solution.py:527
  72.6 2.7 %shard_map.96 = (bf16[64,32,512]{2,1,0:T(8,128)(2,1)}, f32[2,27,32,32]{3,2,1,0:T(8,128)}) custom-call(bf16[64,32,512]{2,1,0:T(8,128)(2,1)} %get-tuple-element.4.moved_in, f32[2,27,32,32]{3,2,1,0:T(8,128)} %get-tuple-element.5.gradients_in), custom_call_target="tpu_custom_call" | custom-call | tf_op jit(solution)/shard_map/pallas_call | solution.py:565

commit v3 on v2

--- a/solution.py
+++ b/solution.py
@@ -154,22 +154,29 @@
     return d, t, (t // 2) * 2, t % 2
 
 
+def flipped(value, bit):
+    step = 2**bit
+    return value + step - 2 * step * ((value // step) % 2)
+
+
 def greet():
     d, t, chip, core = place()
     barrier = pltpu.get_barrier_semaphore()
-
-    def tile_peer(i, carry):
-        pl.semaphore_signal(barrier, inc=1, device_id=(d, (t + i) % TILES), device_id_type=MESH)
-        return carry
-
-    def depth_peer(i, carry):
-        other = ((d + 1 + i // 2) % DEPTHS, chip + i % 2)
-        pl.semaphore_signal(barrier, inc=1, device_id=other, device_id_type=MESH)
-        return carry
-
-    lax.fori_loop(1, TILES, tile_peer, 0)
-    lax.fori_loop(0, 2 * (DEPTHS - 1), depth_peer, 0)
-    return barrier
+    peers = [(d, flipped(t, bit)) for bit in range(5)]
+    peers += [(d, (t + 1) % TILES), (d, (t + TILES - 1) % TILES)]
+    peers += [((d + step) % DEPTHS, t) for step in range(1, DEPTHS)]
+    for peer in peers:
+        pl.semaphore_signal(barrier, inc=1, device_id=peer, device_id_type=MESH)
+    return barrier, len(peers)
+
+
+def spread_word(round_sem, step):
+    d, t, _, _ = place()
+    if step > 0:
+        pl.semaphore_wait(round_sem.at[step - 1], 1)
+    if step < 6:
+        peer = (d, flipped(t, step + 1)) if step < 4 else (flipped(d, step - 4), t)
+        pl.semaphore_signal(round_sem.at[step], inc=1, device_id=peer, device_id_type=MESH)
 
 
 def depth_copies(stage, land, sends, receives):
@@ -243,115 +250,92 @@
 )
 
 
-def shifted_tile(i, sign):
+def shifted_tile(i):
     t = lax.axis_index("tile")
     dy, dx, dc = ORDER[i]
     y, x, core = t // 8, (t // 2) % 4, t % 2
-    return ((y + sign * dy + 4) % 4) * 8 + ((x + sign * dx + 4) % 4) * 2 + (core + dc) % 2
+    return ((y + dy) % 4) * 8 + ((x + dx) % 4) * 2 + (core + dc) % 2
 
 
 def move(i, outgoing, moved, sends, receives):
     d, t = lax.axis_index("depth"), lax.axis_index("tile")
-    peer = shifted_tile(i, 1)
-    return remote(outgoing.at[pl.ds(2 * peer, 2)], moved.at[pl.ds(2 * t, 2)], sends.at[i], receives.at[i], (d, peer))
-
-
-def landed(i, outgoing, moved, sends, receives):
-    d = lax.axis_index("depth")
-    peer = shifted_tile(i, -1)
-    return remote(outgoing.at[pl.ds(2 * peer, 2)], moved.at[pl.ds(2 * peer, 2)], sends.at[i], receives.at[i], (d, peer))
-
-
-def ring_copy(i, source, target, sends, receives, group):
+    peer = shifted_tile(i)
+    return remote(outgoing.at[pl.ds(2 * peer, 2)], moved.at[pl.ds(2 * t, 2)], sends, receives, (d, peer))
+
+
+def ring_copy(i, plan):
+    source, target, _, send, receive, group = plan
     d, t, chip, core = place()
     if group == 8:
         me = d * 2 + core
         peer = (me + i) % 8
         device = (peer // 2, chip + peer % 2)
-    elif group == 16:
+    else:
         me = t // 2
         peer = (me + i) % 16
         device = (d, 2 * peer + core)
-    else:
-        me = t
-        peer = (t + i) % TILES
-        device = (d, peer)
-    return remote(source(me, peer), target(me, peer), sends.at[peer], receives.at[me], device)
-
-
-def arrived_copy(i, source, target, sends, receives, group):
-    d, t, chip, core = place()
-    if group == 8:
-        me = d * 2 + core
-        peer = (me + i) % 8
-        device = (peer // 2, chip + peer % 2)
-    elif group == 16:
-        me = t // 2
-        peer = (me + i) % 16
-        device = (d, 2 * peer + core)
-    else:
-        me = t
-        peer = (t + i) % TILES
-        device = (d, peer)
-    return remote(source(me, peer), target(peer, me), sends.at[peer], receives.at[peer], device)
-
-
-def start_all(*args):
+    return remote(source(me, peer), target(me, peer), send, receive, device)
+
+
+def start_all(plan):
     def step(i, carry):
-        ring_copy(i, *args).start()
+        ring_copy(i, plan).start()
         return carry
 
-    lax.fori_loop(1, args[-1], step, 0)
-
-
-def wait_arrived(*args):
-    def step(i, carry):
-        arrived_copy(i, *args).wait_recv()
-        return carry
-
-    lax.fori_loop(1, args[-1], step, 0)
-
-
-def wait_sent(*args):
-    def step(i, carry):
-        ring_copy(i, *args).wait_send()
-        return carry
-
-    lax.fori_loop(1, args[-1], step, 0)
+    lax.fori_loop(1, plan[-1], step, 0)
+
+
+def all_of(whole, send, receive):
+    d, t, _, _ = place()
+    return remote(whole, whole, send, receive, (d, (t + 1) % TILES))
+
+
+def wait_arrived(plan):
+    all_of(plan[2], plan[3], plan[4]).wait_recv()
+
+
+def wait_sent(plan):
+    all_of(plan[2], plan[3], plan[4]).wait_send()
 
 
 def reduce_plans(packed, land_a, part, land_b, result, sems):
     a_send, a_receive, b_send, b_receive, c_send, c_receive = sems
-    first = (lambda me, peer: packed.at[pl.ds(4 * peer, 4)], lambda me, peer: land_a.at[me], a_send, a_receive, 8)
-    second = (lambda me, peer: part, lambda me, peer: land_b.at[me], b_send, b_receive, 16)
-    third = (lambda me, peer: land_b.at[16], lambda me, peer: result.at[pl.ds(4 * me, 4)], c_send, c_receive, 8)
+    first = (
+        lambda me, peer: packed.at[pl.ds(4 * peer, 4)], lambda me, peer: land_a.at[me], land_a.at[pl.ds(0, 7)],
+        a_send, a_receive, 8,
+    )
+    second = (lambda me, peer: part, lambda me, peer: land_b.at[me], land_b.at[pl.ds(0, 15)], b_send, b_receive, 16)
+    third = (
+        lambda me, peer: land_b.at[16], lambda me, peer: result.at[pl.ds(4 * me, 4)], result.at[pl.ds(0, 28)],
+        c_send, c_receive, 8,
+    )
     return first, second, third
 
 
 def reduce_first(plans, packed, land_a, part, land_b):
     d, t, chip, core = place()
     me = d * 2 + core
-    wait_arrived(*plans[0])
+    wait_arrived(plans[0])
     land_a[me] = packed[pl.ds(4 * me, 4)]
     total = land_a[0]
     for j in range(1, 8):
         total += land_a[j]
     part[...] = total
     land_b[t // 2] = total
-    start_all(*plans[1])
+    start_all(plans[1])
 
 
 def reduce_second(plans, part, land_b, result, factor):
     d, t, chip, core = place()
     me = d * 2 + core
-    wait_arrived(*plans[1])
+    wait_arrived(plans[1])
     total = land_b[0]
     for j in range(1, 16):
         total += land_b[j]
     total = total * factor
     land_b[16] = total
     result[pl.ds(4 * me, 4)] = total
-    start_all(*plans[2])
+    start_all(plans[2])
 
 
 def unpack_gradient(result, out, w):
@@ -373,7 +357,7 @@
     stage_d2, land_d2, stage_t2, land_t2, sections2,
     packed, land_a, part, land_b, result,
     d_send, d_receive, t_send, t_receive, d2_send, d2_receive, t2_send, t2_receive,
-    load_sem, store_sem, m_send, m_receive, own_sem, a_send, a_receive, b_send, b_receive, c_send, c_receive,
+    load_sem, store_sem, m_send, m_receive, own_sem, a_send, a_receive, b_send, b_receive, c_send, c_receive, round_sem,
 ):
     d, t, chip, core = place()
     fields, tables = (features, cotangent), (table_x, table_g)
@@ -384,11 +368,11 @@
     loads = [pltpu.make_async_copy(source, target, load_sem.at[i]) for i, (source, target) in enumerate(pairs)]
     for load in loads:
         load.start()
-    barrier = greet()
+    barrier, greetings = greet()
     for load in loads:
         load.wait()
     stage_depth(fields, send_depth, stage_d)
-    pl.semaphore_wait(barrier, TILES - 1 + 2 * (DEPTHS - 1))
+    pl.semaphore_wait(barrier, greetings)
     along_depth = depth_copies(stage_d, land_d, d_send, d_receive)
     for copy in along_depth:
         copy.start()
@@ -396,6 +380,7 @@
     table_x[16] = jnp.zeros((64, 8, 128), F32)
     table_g[16] = jnp.zeros((64, 8, 128), F32)
     spread_weight(first_weight, wide_first)
+    spread_word(round_sem, 0)
     for copy in along_depth:
         copy.wait()
     accept_depth(fields, land_d, sections, tables)
@@ -405,15 +390,20 @@
         copy.start()
     table_depth(sections, tables)
     spread_weight(second_weight, wide_second)
+    spread_word(round_sem, 1)
     for copy in along_tile:
         copy.wait()
     table_tile(land_t, tables)
     build_shifts(table_x, links, even_x, odd_x)
+    spread_word(round_sem, 2)
     build_shifts(table_g, links, even_g, odd_g)
+    spread_word(round_sem, 3)
     pre[...] = jnp.zeros((512, 256), F32)
     back[...] = jnp.zeros((512, 256), F32)
     conv_forward(even_x, odd_x, wide_first, pre)
+    spread_word(round_sem, 4)
     conv_backward(even_g, odd_g, wide_second, back)
+    spread_word(round_sem, 5)
     value = pre[...]
     sigma = 1.0 / (1.0 + jnp.exp(-value))
     hidden[...] = (value * sigma).T.astype(BF16)
@@ -424,6 +414,7 @@
     for copy in along_depth:
         copy.start()
     weight_gradient(lambda: hidden[...], even_g, odd_g, folded)
+    spread_word(round_sem, 6)
     for copy in along_depth:
         copy.wait()
     accept_depth((grad_pre,), land_d2, sections2, tables)
@@ -439,7 +430,7 @@
         )
         for w in range(2)
     ]
-    start_all(*plans[1][0])
+    start_all(plans[1][0])
     table_own((grad_pre,), tables[:1])
     table_depth(sections2, tables[:1])
     for copy in along_tile:
@@ -475,29 +466,29 @@
         move(i, outgoing, moved, m_send, m_receive).start()
     weight_gradient(lambda: features[...].reshape(256, 512), even_x, odd_x, folded)
     pack_gradient(folded, packed.at[0])
-    start_all(*plans[0][0])
+    start_all(plans[0][0])
     for i in range(10, 17):
         move(i, outgoing, moved, m_send, m_receive).start()
     reduce_second(plans[1], part.at[1], land_b.at[1], result.at[1], factor)
     reduce_first(plans[0], packed.at[0], land_a.at[0], part.at[0], land_b.at[0])
     for i in range(17, 24):
         move(i, outgoing, moved, m_send, m_receive).start()
-    wait_arrived(*plans[1][2])
+    wait_arrived(plans[1][2])
     unpack_gradient(result.at[1], gradients, 1)
     reduce_second(plans[0], part.at[0], land_b.at[0], result.at[0], factor)
     for i in range(24, 31):
         move(i, outgoing, moved, m_send, m_receive).start()
-    wait_arrived(*plans[0][2])
+    wait_arrived(plans[0][2])
     unpack_gradient(result.at[0], gradients, 0)
     store = pltpu.make_async_copy(gradients, gradients_out, store_sem)
     store.start()
     for w in range(2):
         for plan in plans[w]:
-            wait_sent(*plan)
+            wait_sent(plan)
     own.wait()
-    for i in range(31):
-        landed(i, outgoing, moved, m_send, m_receive).wait_recv()
-        move(i, outgoing, moved, m_send, m_receive).wait_send()
+    whole = all_of(moved.at[pl.ds(0, 62)], m_send, m_receive)
+    whole.wait_recv()
+    whole.wait_send()
     store.wait()
 
 
@@ -553,11 +544,9 @@
         ]
         + [dma((2,))] * 8
         + [dma((8,)), dma]
-        + [dma((TILES - 1,))] * 2
-        + [dma]
-        + [dma((2, 8))] * 2
-        + [dma((2, 16))] * 2
-        + [dma((2, 8))] * 2,
+        + [dma] * 3
+        + [dma((2,))] * 6
+        + [pltpu.SemaphoreType.REGULAR((6,))],
         compiler_params=pltpu.CompilerParams(
             collective_id=0, has_side_effects=True, vmem_limit_bytes=64 * 2**20 - 2**17
         ),

time: 75.5 us -> 71 us (0.940)
  Pallas kernels: 74.7 us -> 70.2 us
    pallas_call x1, Pallas kernels: 72 us -> 67.4 us  [local(): pl.pallas_call(kernel, out_shape=(jax.ShapeDtypeStruct((2 * TILES, *brick...]
where the time goes in v3:
time: 71 us; the launch traced here: 70.8 us
  Pallas kernels  70.2 us (99%)
    pallas_call x1, Pallas kernels, local(): pl.pallas_call(kernel, out_shape=(jax.ShapeDtypeStruct((2 * TILES, *brick...  67.4 us
    pallas_call x1, Pallas kernels, local(): pl.pallas_call(hand_over, out_shape=tuple((jax.ShapeDtypeStruct(r.shape,...  2.73 us

profile of v3, /device:TPU:1, one launch (start us, length us, event | category | flops | bytes accessed | tf_op | source)
XLA Modules:
  0.0 70.8 jit_solution(4220126858830025508)
XLA Ops:
  0.6 67.4 %shard_map.95 = (bf16[64,32,512]{2,1,0:T(8,128)(2,1)}, f32[2,27,32,32]{3,2,1,0:T(8,128)}) custom-call(bf16[8,32,512]{2,1,0:T(8,128)(2,1)} %features_in.1, bf16[8,32,512]{2,1,0:T(8,128)(2,1)} %cotangent_in.1, bf16[27,32,32]{2,1,0:T(8,128)(2,1)} %first_in.1, bf16[27,32,32]{2,1,0:T(8,128)(2,1)} %second_in.1, s32[8,26]{1,0:T(8,128)} %links_in.1, ...), custom_call_target="tpu_custom_call" | custom-call | tf_op jit(solution)/shard_map/pallas_call | solution.py:518
  68.1 2.7 %shard_map.96 = (bf16[64,32,512]{2,1,0:T(8,128)(2,1)}, f32[2,27,32,32]{3,2,1,0:T(8,128)}) custom-call(bf16[64,32,512]{2,1,0:T(8,128)(2,1)} %get-tuple-element.4.moved_in, f32[2,27,32,32]{3,2,1,0:T(8,128)} %get-tuple-element.5.gradients_in), custom_call_target="tpu_custom_call" | custom-call | tf_op jit(solution)/shard_map/pallas_call | solution.py:554

commit v4 on v3

--- a/solution.py
+++ b/solution.py
@@ -240,27 +240,83 @@
                 fill_table(table, 12 + 2 * side + j, land[side, 2 * f + j])
 
 
-ORDER = (
-    (1, 2, 1), (3, 1, 0), (0, 3, 1), (2, 2, 0), (0, 0, 1), (1, 3, 0),
-    (3, 1, 1), (1, 0, 0), (2, 2, 1), (0, 1, 0), (1, 3, 1), (3, 2, 0),
-    (1, 0, 1), (2, 3, 0), (0, 1, 1), (2, 0, 0), (3, 2, 1), (1, 1, 0),
-    (2, 3, 1), (0, 2, 0), (2, 0, 1), (3, 3, 0), (1, 1, 1), (3, 0, 0),
-    (0, 2, 1), (2, 1, 0), (3, 3, 1), (1, 2, 0), (3, 0, 1), (0, 3, 0),
-    (2, 1, 1),
-)
-
-
-def shifted_tile(i):
+def line_tile(axis, step, turn=0):
     t = lax.axis_index("tile")
-    dy, dx, dc = ORDER[i]
+    y, x, core = t // 8, (t // 2) % 4, (t + turn) % 2
+    if axis == 0:
+        return y * 8 + ((x + step) % 4) * 2 + core
+    return ((y + step) % 4) * 8 + x * 2 + core
+
+
+def line_place(axis):
+    t = lax.axis_index("tile")
+    return (t // 2) % 4 if axis == 0 else t // 8
+
+
+def share_workers(workers_in, names_land, sends, receives, own_sems):
+    d = lax.axis_index("depth")
+    remotes, owns = [], []
+    for axis in range(2):
+        slot = names_land.at[4 * axis + line_place(axis)]
+        owns.append(pltpu.make_async_copy(workers_in, slot, own_sems.at[axis]))
+        for step in (1, 2, 3):
+            remotes.append(remote(workers_in, slot, sends, receives, (d, line_tile(axis, step))))
+    return remotes, owns
+
+
+def broadcast_copy(axis, step, grad_input, gather, sends, receives):
+    d = lax.axis_index("depth")
+    return remote(
+        grad_input.at[pl.ds(0, 8), pl.ds(16 * axis, 16)],
+        gather.at[axis, line_place(axis), pl.ds(0, 8)],
+        sends.at[axis],
+        receives.at[axis],
+        (d, line_tile(axis, step)),
+    )
+
+
+def find_slots(names, slots):
+    for line in range(8):
+        own = [names[line, 0, n] for n in range(8)]
+        for n in range(8):
+            rank = jnp.int32(0)
+            for m in range(n):
+                rank = rank + jnp.where(own[m] == own[n], 1, 0)
+            slots[line, n] = 2 * own[n] + rank
+
+
+def fill_message(axis, index, target, gather, slots, outgoing):
+    for source in range(4):
+        held = [slots[4 * axis + source, n] for n in range(8)]
+        for q in range(2):
+            key = 2 * target + q
+            brick = jnp.int32(8)
+            for n in range(8):
+                brick = jnp.where(held[n] == key, n, brick)
+            outgoing[axis, index, source, q] = gather[axis, source, brick]
+
+
+def message_target(axis, moved):
+    t = lax.axis_index("tile")
     y, x, core = t // 8, (t // 2) % 4, t % 2
-    return ((y + dy) % 4) * 8 + ((x + dx) % 4) * 2 + (core + dc) % 2
-
-
-def move(i, outgoing, moved, sends, receives):
-    d, t = lax.axis_index("depth"), lax.axis_index("tile")
-    peer = shifted_tile(i)
-    return remote(outgoing.at[pl.ds(2 * peer, 2)], moved.at[pl.ds(2 * t, 2)], sends, receives, (d, peer))
+    if axis == 0:
+        return moved.at[y, pl.ds(0, 4), core, pl.ds(0, 2), pl.ds(0, 16)]
+    return moved.at[pl.ds(0, 4), x, core, pl.ds(0, 2), pl.ds(16, 16)]
+
+
+def send_messages(steps, gather, slots, outgoing, moved, sends, receives, own_sems):
+    d = lax.axis_index("depth")
+    for step in steps:
+        for axis in range(2):
+            for turn in range(2):
+                index = 2 * step + turn
+                target = line_tile(1 - axis, step, turn)
+                fill_message(axis, index, target, gather, slots, outgoing)
+                source = outgoing.at[axis, index]
+                if index == 0:
+                    pltpu.make_async_copy(source, message_target(axis, moved), own_sems.at[axis]).start()
+                else:
+                    remote(source, message_target(axis, moved), sends.at[axis], receives.at[axis], (d, target)).start()
 
 
 def ring_copy(i, plan):
@@ -350,20 +406,20 @@
 def kernel(
     features_in, cotangent_in, first_in, second_in, links_in, depth_in, tile_in, workers_in,
     moved, gradients_out,
-    features, cotangent, first_weight, second_weight, links, send_depth, send_tile, workers, gradients,
+    features, cotangent, first_weight, second_weight, links, send_depth, send_tile, gradients,
     table_x, table_g, even_x, odd_x, even_g, odd_g, wide_first, wide_second, pre, back, hidden, folded,
-    grad_pre, grad_input, outgoing,
+    grad_pre, grad_input, gather, outgoing, names_land, names, slots,
     stage_d, land_d, stage_t, land_t, sections,
     stage_d2, land_d2, stage_t2, land_t2, sections2,
     packed, land_a, part, land_b, result,
     d_send, d_receive, t_send, t_receive, d2_send, d2_receive, t2_send, t2_receive,
-    load_sem, store_sem, m_send, m_receive, own_sem, a_send, a_receive, b_send, b_receive, c_send, c_receive, round_sem,
+    load_sem, store_sem, m_send, m_receive, own_sem, g_send, g_receive, n_send, n_receive, n_own, n_sem, a_send, a_receive, b_send, b_receive, c_send, c_receive, round_sem,
 ):
     d, t, chip, core = place()
     fields, tables = (features, cotangent), (table_x, table_g)
     pairs = (
         (features_in, features), (cotangent_in, cotangent), (depth_in, send_depth), (tile_in, send_tile),
-        (links_in, links), (workers_in, workers), (first_in, first_weight), (second_in, second_weight),
+        (links_in, links), (first_in, first_weight), (second_in, second_weight),
     )
     loads = [pltpu.make_async_copy(source, target, load_sem.at[i]) for i, (source, target) in enumerate(pairs)]
     for load in loads:
@@ -415,6 +471,9 @@
         copy.start()
     weight_gradient(lambda: hidden[...], even_g, odd_g, folded)
     spread_word(round_sem, 6)
+    remotes, owns = share_workers(workers_in, names_land, n_send, n_receive, n_own)
+    for copy in remotes + owns:
+        copy.start()
     for copy in along_depth:
         copy.wait()
     accept_depth((grad_pre,), land_d2, sections2, tables)
@@ -440,44 +499,38 @@
     back[...] = jnp.zeros((512, 256), F32)
     conv_backward(even_x, odd_x, wide_first, back)
     reduce_first(plans[1], packed.at[1], land_a.at[1], part.at[1], land_b.at[1])
-    grad_input[0:8] = (back[...].T.reshape(8, 32, 512) + cotangent[...].astype(F32)).astype(BF16)
-    grad_input[8] = jnp.zeros((32, 512), BF16)
-
-    names = [workers[0, n] for n in range(8)]
-    slots = []
-    for n in range(8):
-        rank = jnp.int32(0)
-        for m in range(n):
-            rank = rank + jnp.where(names[m] == names[n], 1, 0)
-        slots.append(2 * names[n] + rank)
-
-    def place_brick(s, carry):
-        brick = jnp.int32(8)
-        for n in range(8):
-            brick = jnp.where(slots[n] == s, n, brick)
-        outgoing[s] = grad_input[brick]
-        return carry
-
-    lax.fori_loop(0, 2 * TILES, place_brick, 0)
-    own = pltpu.make_async_copy(outgoing.at[pl.ds(2 * t, 2)], moved.at[pl.ds(2 * t, 2)], own_sem)
-    own.start()
+    grad_input[...] = (back[...].T.reshape(8, 32, 512) + cotangent[...].astype(F32)).astype(BF16)
+    for step in (1, 3, 2):
+        for axis in range(2):
+            broadcast_copy(axis, step, grad_input, gather, g_send, g_receive).start()
+    for axis in range(2):
+        gather[axis, line_place(axis), 0:8] = grad_input[:, 16 * axis : 16 * axis + 16]
+        for source in range(4):
+            gather[axis, source, 8] = jnp.zeros((16, 512), BF16)
+    all_names = all_of(names_land.at[pl.ds(0, 6)], n_send, n_receive)
+    all_names.wait_recv()
+    for copy in owns:
+        copy.wait()
+    to_scalar = pltpu.make_async_copy(names_land, names, n_sem)
+    to_scalar.start()
+    to_scalar.wait()
+    find_slots(names, slots)
+
     factor = float(DEPTHS * TILES * 8 * 512) ** (-0.5)
-    for i in range(0, 10):
-        move(i, outgoing, moved, m_send, m_receive).start()
     weight_gradient(lambda: features[...].reshape(256, 512), even_x, odd_x, folded)
     pack_gradient(folded, packed.at[0])
     start_all(plans[0][0])
-    for i in range(10, 17):
-        move(i, outgoing, moved, m_send, m_receive).start()
+    for axis in range(2):
+        all_of(gather.at[axis, pl.ds(0, 3), pl.ds(0, 8)], g_send.at[axis], g_receive.at[axis]).wait_recv()
+    parts = (gather, slots, outgoing, moved, m_send, m_receive, own_sem)
+    send_messages((2,), *parts)
     reduce_second(plans[1], part.at[1], land_b.at[1], result.at[1], factor)
     reduce_first(plans[0], packed.at[0], land_a.at[0], part.at[0], land_b.at[0])
-    for i in range(17, 24):
-        move(i, outgoing, moved, m_send, m_receive).start()
+    send_messages((1, 3), *parts)
     wait_arrived(plans[1][2])
     unpack_gradient(result.at[1], gradients, 1)
     reduce_second(plans[0], part.at[0], land_b.at[0], result.at[0], factor)
-    for i in range(24, 31):
-        move(i, outgoing, moved, m_send, m_receive).start()
+    send_messages((0,), *parts)
     wait_arrived(plans[0][2])
     unpack_gradient(result.at[0], gradients, 0)
     store = pltpu.make_async_copy(gradients, gradients_out, store_sem)
@@ -485,10 +538,13 @@
     for w in range(2):
         for plan in plans[w]:
             wait_sent(plan)
-    own.wait()
-    whole = all_of(moved.at[pl.ds(0, 62)], m_send, m_receive)
-    whole.wait_recv()
-    whole.wait_send()
+    all_names.wait_send()
+    for axis in range(2):
+        all_of(gather.at[axis, pl.ds(0, 3), pl.ds(0, 8)], g_send.at[axis], g_receive.at[axis]).wait_send()
+        pltpu.make_async_copy(outgoing.at[axis, 0], message_target(axis, moved), own_sem.at[axis]).wait()
+        messages = all_of(outgoing.at[axis, pl.ds(1, 7)], m_send.at[axis], m_receive.at[axis])
+        messages.wait_send()
+        messages.wait_recv()
     store.wait()
 
 
@@ -518,21 +574,23 @@
     results = pl.pallas_call(
         kernel,
         out_shape=(
-            jax.ShapeDtypeStruct((2 * TILES, *brick), BF16),
+            jax.ShapeDtypeStruct((4, 4, 2, 2, *brick), BF16),
             jax.ShapeDtypeStruct((2, 27, 32, 32), F32),
         ),
         in_specs=[anywhere] * 8,
         out_specs=(anywhere, anywhere),
         scratch_shapes=[pltpu.VMEM((8, *brick), BF16)] * 2
         + [pltpu.VMEM((27, 32, 32), BF16)] * 2
-        + [pltpu.SMEM((8, 26), jnp.int32), pltpu.SMEM((1, 2, 2), jnp.int32), pltpu.SMEM((1, 2, 2), jnp.int32), pltpu.SMEM((1, 8), jnp.int32)]
+        + [pltpu.SMEM((8, 26), jnp.int32), pltpu.SMEM((1, 2, 2), jnp.int32), pltpu.SMEM((1, 2, 2), jnp.int32)]
         + [pltpu.VMEM((2, 27, 32, 32), F32)]
         + [pltpu.VMEM((17, 64, 8, 128), F32)] * 2
         + shifts * 2
         + [pltpu.VMEM((3, 2304, 256), BF16)] * 2
         + [pltpu.VMEM((512, 256), F32)] * 2
         + [pltpu.VMEM((256, 512), BF16), pltpu.VMEM((864, 128), F32)]
-        + [pltpu.VMEM((8, *brick), BF16), pltpu.VMEM((9, *brick), BF16), pltpu.VMEM((64, *brick), BF16)]
+        + [pltpu.VMEM((8, *brick), BF16), pltpu.VMEM((8, *brick), BF16)]
+        + [pltpu.VMEM((2, 4, 9, 16, 512), BF16), pltpu.VMEM((2, 8, 4, 2, 16, 512), BF16)]
+        + [pltpu.VMEM((8, 1, 8), jnp.int32), pltpu.SMEM((8, 1, 8), jnp.int32), pltpu.SMEM((8, 8), jnp.int32)]
         + halo(2)
         + halo(1)
         + [
@@ -543,14 +601,16 @@
             pltpu.VMEM((2, 32, 8, 128), F32),
         ]
         + [dma((2,))] * 8
-        + [dma((8,)), dma]
-        + [dma] * 3
+        + [dma((7,)), dma]
+        + [dma((2,))] * 5
+        + [dma, dma, dma((2,)), dma]
         + [dma((2,))] * 6
         + [pltpu.SemaphoreType.REGULAR((6,))],
         compiler_params=pltpu.CompilerParams(
             collective_id=0, has_side_effects=True, vmem_limit_bytes=64 * 2**20 - 2**17
         ),
     )(features, cotangent, first_weight, second_weight, neighbours, send_depth, send_tile, worker_tile.reshape(1, 8))
+    results = (results[0].reshape(2 * TILES, *brick), results[1])
     return pl.pallas_call(
         hand_over,
         out_shape=tuple(jax.ShapeDtypeStruct(r.shape, r.dtype) for r in results),

time: 71 us -> 67 us (0.944)
  Pallas kernels: 70.2 us -> 66.2 us
    pallas_call x1, Pallas kernels: 67.4 us -> 63.4 us  [local(): pl.pallas_call(kernel, out_shape=(jax.ShapeDtypeStruct((4, 4, 2, 2, *bric...]
where the time goes in v4:
time: 67 us; the launch traced here: 66.8 us
  Pallas kernels  66.2 us (99%)
    pallas_call x1, Pallas kernels, local(): pl.pallas_call(kernel, out_shape=(jax.ShapeDtypeStruct((4, 4, 2, 2, *bric...  63.4 us
    pallas_call x1, Pallas kernels, local(): pl.pallas_call(hand_over, out_shape=tuple((jax.ShapeDtypeStruct(r.shape,...  2.73 us

profile of v4, /device:TPU:1, one launch (start us, length us, event | category | flops | bytes accessed | tf_op | source)
XLA Modules:
  0.0 66.8 jit_solution(12815687721470304321)
XLA Ops:
  0.6 63.4 %shard_map.95 = (bf16[4,4,2,2,32,512]{5,4,3,2,1,0:T(8,128)(2,1)}, f32[2,27,32,32]{3,2,1,0:T(8,128)}) custom-call(bf16[8,32,512]{2,1,0:T(8,128)(2,1)} %features_in.1, bf16[8,32,512]{2,1,0:T(8,128)(2,1)} %cotangent_in.1, bf16[27,32,32]{2,1,0:T(8,128)(2,1)} %first_in.1, bf16[27,32,32]{2,1,0:T(8,128)(2,1)} %second_in.1, s32[8,26]{1,0:T(8,128)} %links_in.1, ...), custom_call_target="tpu_custom_call" | custom-call | tf_op jit(solution)/shard_map/pallas_call | solution.py:574
  64.1 2.7 %shard_map.96 = (bf16[64,32,512]{2,1,0:T(8,128)(2,1)}, f32[2,27,32,32]{3,2,1,0:T(8,128)}) custom-call(bf16[64,32,512]{2,1,0:T(8,128)(2,1)} %bitcast.2, f32[2,27,32,32]{3,2,1,0:T(8,128)} %get-tuple-element.5.gradients_in), custom_call_target="tpu_custom_call" | custom-call | tf_op jit(solution)/shard_map/pallas_call | solution.py:614

commit v5 on v4

--- a/solution.py
+++ b/solution.py
@@ -410,9 +410,10 @@
     table_x, table_g, even_x, odd_x, even_g, odd_g, wide_first, wide_second, pre, back, hidden, folded,
     grad_pre, grad_input, gather, outgoing, names_land, names, slots,
     stage_d, land_d, stage_t, land_t, sections,
+    stage_d1, land_d1, stage_t1, land_t1, sections1,
     stage_d2, land_d2, stage_t2, land_t2, sections2,
     packed, land_a, part, land_b, result,
-    d_send, d_receive, t_send, t_receive, d2_send, d2_receive, t2_send, t2_receive,
+    d_send, d_receive, t_send, t_receive, d1_send, d1_receive, t1_send, t1_receive, d2_send, d2_receive, t2_send, t2_receive,
     load_sem, store_sem, m_send, m_receive, own_sem, g_send, g_receive, n_send, n_receive, n_own, n_sem, a_send, a_receive, b_send, b_receive, c_send, c_receive, round_sem,
 ):
     d, t, chip, core = place()
@@ -427,43 +428,57 @@
     barrier, greetings = greet()
     for load in loads:
         load.wait()
-    stage_depth(fields, send_depth, stage_d)
+    stage_depth((features,), send_depth, stage_d)
+    stage_depth((cotangent,), send_depth, stage_d1)
     pl.semaphore_wait(barrier, greetings)
-    along_depth = depth_copies(stage_d, land_d, d_send, d_receive)
-    for copy in along_depth:
+    depth_x = depth_copies(stage_d, land_d, d_send, d_receive)
+    depth_g = depth_copies(stage_d1, land_d1, d1_send, d1_receive)
+    for copy in depth_x + depth_g:
         copy.start()
     table_own(fields, tables)
     table_x[16] = jnp.zeros((64, 8, 128), F32)
     table_g[16] = jnp.zeros((64, 8, 128), F32)
+    spread_word(round_sem, 0)
+    for copy in depth_x:
+        copy.wait()
+    accept_depth((features,), land_d, sections, tables)
+    stage_tile(1, sections, send_tile, stage_t)
+    tile_x = tile_copies(stage_t, land_t, t_send, t_receive)
+    for copy in tile_x:
+        copy.start()
+    table_depth(sections, tables[:1])
     spread_weight(first_weight, wide_first)
-    spread_word(round_sem, 0)
-    for copy in along_depth:
+    for copy in depth_g:
         copy.wait()
-    accept_depth(fields, land_d, sections, tables)
-    stage_tile(2, sections, send_tile, stage_t)
-    along_tile = tile_copies(stage_t, land_t, t_send, t_receive)
-    for copy in along_tile:
+    accept_depth((cotangent,), land_d1, sections1, tables)
+    stage_tile(1, sections1, send_tile, stage_t1)
+    tile_g = tile_copies(stage_t1, land_t1, t1_send, t1_receive)
+    for copy in tile_g:
         copy.start()
-    table_depth(sections, tables)
-    spread_weight(second_weight, wide_second)
     spread_word(round_sem, 1)
-    for copy in along_tile:
+    table_depth(sections1, tables[1:])
+    for copy in tile_x:
         copy.wait()
-    table_tile(land_t, tables)
+    table_tile(land_t, tables[:1])
     build_shifts(table_x, links, even_x, odd_x)
     spread_word(round_sem, 2)
-    build_shifts(table_g, links, even_g, odd_g)
-    spread_word(round_sem, 3)
     pre[...] = jnp.zeros((512, 256), F32)
     back[...] = jnp.zeros((512, 256), F32)
     conv_forward(even_x, odd_x, wide_first, pre)
+    spread_word(round_sem, 3)
+    spread_weight(second_weight, wide_second)
+    value = pre[...]
+    sigma = 1.0 / (1.0 + jnp.exp(-value))
+    hidden[...] = (value * sigma).T.astype(BF16)
+    pre[...] = sigma * (1.0 + value * (1.0 - sigma))
+    for copy in tile_g:
+        copy.wait()
+    table_tile(land_t1, tables[1:])
+    build_shifts(table_g, links, even_g, odd_g)
     spread_word(round_sem, 4)
     conv_backward(even_g, odd_g, wide_second, back)
     spread_word(round_sem, 5)
-    value = pre[...]
-    sigma = 1.0 / (1.0 + jnp.exp(-value))
-    hidden[...] = (value * sigma).T.astype(BF16)
-    grad_pre[...] = (back[...] * sigma * (1.0 + value * (1.0 - sigma))).T.astype(BF16).reshape(8, 32, 512)
+    grad_pre[...] = (back[...] * pre[...]).T.astype(BF16).reshape(8, 32, 512)
 
     stage_depth((grad_pre,), send_depth, stage_d2)
     along_depth = depth_copies(stage_d2, land_d2, d2_send, d2_receive)
@@ -498,7 +513,6 @@
     build_shifts(table_x, links, even_x, odd_x)
     back[...] = jnp.zeros((512, 256), F32)
     conv_backward(even_x, odd_x, wide_first, back)
-    reduce_first(plans[1], packed.at[1], land_a.at[1], part.at[1], land_b.at[1])
     grad_input[...] = (back[...].T.reshape(8, 32, 512) + cotangent[...].astype(F32)).astype(BF16)
     for step in (1, 3, 2):
         for axis in range(2):
@@ -517,6 +531,7 @@
     find_slots(names, slots)
 
     factor = float(DEPTHS * TILES * 8 * 512) ** (-0.5)
+    reduce_first(plans[1], packed.at[1], land_a.at[1], part.at[1], land_b.at[1])
     weight_gradient(lambda: features[...].reshape(256, 512), even_x, odd_x, folded)
     pack_gradient(folded, packed.at[0])
     start_all(plans[0][0])
@@ -591,7 +606,8 @@
         + [pltpu.VMEM((8, *brick), BF16), pltpu.VMEM((8, *brick), BF16)]
         + [pltpu.VMEM((2, 4, 9, 16, 512), BF16), pltpu.VMEM((2, 8, 4, 2, 16, 512), BF16)]
         + [pltpu.VMEM((8, 1, 8), jnp.int32), pltpu.SMEM((8, 1, 8), jnp.int32), pltpu.SMEM((8, 8), jnp.int32)]
-        + halo(2)
+        + halo(1)
+        + halo(1)
         + halo(1)
         + [
             pltpu.VMEM((2, 32, 8, 128), F32),
@@ -600,7 +616,7 @@
             pltpu.VMEM((2, 17, 4, 8, 128), F32),
             pltpu.VMEM((2, 32, 8, 128), F32),
         ]
-        + [dma((2,))] * 8
+        + [dma((2,))] * 12
         + [dma((7,)), dma]
         + [dma((2,))] * 5
         + [dma, dma, dma((2,)), dma]

time: 67 us -> 65.5 us (0.978)
  Pallas kernels: 66.2 us -> 64.7 us
    pallas_call x1, Pallas kernels: 63.4 us -> 61.9 us  [local(): pl.pallas_call(kernel, out_shape=(jax.ShapeDtypeStruct((4, 4, 2, 2, *bric...]
where the time goes in v5:
time: 65.5 us; the launch traced here: 65.3 us
  Pallas kernels  64.7 us (99%)
    pallas_call x1, Pallas kernels, local(): pl.pallas_call(kernel, out_shape=(jax.ShapeDtypeStruct((4, 4, 2, 2, *bric...  61.9 us
    pallas_call x1, Pallas kernels, local(): pl.pallas_call(hand_over, out_shape=tuple((jax.ShapeDtypeStruct(r.shape,...  2.73 us

profile of v5, /device:TPU:1, one launch (start us, length us, event | category | flops | bytes accessed | tf_op | source)
XLA Modules:
  0.0 65.3 jit_solution(12362857268928830926)
XLA Ops:
  0.6 61.9 %shard_map.95 = (bf16[4,4,2,2,32,512]{5,4,3,2,1,0:T(8,128)(2,1)}, f32[2,27,32,32]{3,2,1,0:T(8,128)}) custom-call(bf16[8,32,512]{2,1,0:T(8,128)(2,1)} %features_in.1, bf16[8,32,512]{2,1,0:T(8,128)(2,1)} %cotangent_in.1, bf16[27,32,32]{2,1,0:T(8,128)(2,1)} %first_in.1, bf16[27,32,32]{2,1,0:T(8,128)(2,1)} %second_in.1, s32[8,26]{1,0:T(8,128)} %links_in.1, ...), custom_call_target="tpu_custom_call" | custom-call | tf_op jit(solution)/shard_map/pallas_call | solution.py:589
  62.6 2.7 %shard_map.96 = (bf16[64,32,512]{2,1,0:T(8,128)(2,1)}, f32[2,27,32,32]{3,2,1,0:T(8,128)}) custom-call(bf16[64,32,512]{2,1,0:T(8,128)(2,1)} %bitcast.2, f32[2,27,32,32]{3,2,1,0:T(8,128)} %get-tuple-element.5.gradients_in), custom_call_target="tpu_custom_call" | custom-call | tf_op jit(solution)/shard_map/pallas_call | solution.py:630

commit v6 on v5

--- a/solution.py
+++ b/solution.py
@@ -514,7 +514,7 @@
     back[...] = jnp.zeros((512, 256), F32)
     conv_backward(even_x, odd_x, wide_first, back)
     grad_input[...] = (back[...].T.reshape(8, 32, 512) + cotangent[...].astype(F32)).astype(BF16)
-    for step in (1, 3, 2):
+    for step in (2, 1, 3):
         for axis in range(2):
             broadcast_copy(axis, step, grad_input, gather, g_send, g_receive).start()
     for axis in range(2):

time: 65.5 us -> 64.2 us (0.980)
  Pallas kernels: 64.7 us -> 63.3 us
    pallas_call x1, Pallas kernels: 61.9 us -> 60.6 us  [local(): pl.pallas_call(kernel, out_shape=(jax.ShapeDtypeStruct((4, 4, 2, 2, *bric...]
where the time goes in v6:
time: 64.2 us; the launch traced here: 64 us
  Pallas kernels  63.3 us (99%)
    pallas_call x1, Pallas kernels, local(): pl.pallas_call(kernel, out_shape=(jax.ShapeDtypeStruct((4, 4, 2, 2, *bric...  60.6 us
    pallas_call x1, Pallas kernels, local(): pl.pallas_call(hand_over, out_shape=tuple((jax.ShapeDtypeStruct(r.shape,...  2.73 us

profile of v6, /device:TPU:1, one launch (start us, length us, event | category | flops | bytes accessed | tf_op | source)
XLA Modules:
  0.0 64.0 jit_solution(4414491221367561144)
XLA Ops:
  0.6 60.6 %shard_map.95 = (bf16[4,4,2,2,32,512]{5,4,3,2,1,0:T(8,128)(2,1)}, f32[2,27,32,32]{3,2,1,0:T(8,128)}) custom-call(bf16[8,32,512]{2,1,0:T(8,128)(2,1)} %features_in.1, bf16[8,32,512]{2,1,0:T(8,128)(2,1)} %cotangent_in.1, bf16[27,32,32]{2,1,0:T(8,128)(2,1)} %first_in.1, bf16[27,32,32]{2,1,0:T(8,128)(2,1)} %second_in.1, s32[8,26]{1,0:T(8,128)} %links_in.1, ...), custom_call_target="tpu_custom_call" | custom-call | tf_op jit(solution)/shard_map/pallas_call | solution.py:589
  61.3 2.7 %shard_map.96 = (bf16[64,32,512]{2,1,0:T(8,128)(2,1)}, f32[2,27,32,32]{3,2,1,0:T(8,128)}) custom-call(bf16[64,32,512]{2,1,0:T(8,128)(2,1)} %bitcast.2, f32[2,27,32,32]{3,2,1,0:T(8,128)} %get-tuple-element.5.gradients_in), custom_call_target="tpu_custom_call" | custom-call | tf_op jit(solution)/shard_map/pallas_call | solution.py:630
